TPU v7x, 256 devices: a whole 4x4x8 slice. The times are simulated.
256 devices in a mesh: dp: 32 (over x, z), fsdp: 8 (over y, core).
Axes of the slice: x: 4, y: 4, z: 8, core: 2. Of those that a mesh axis runs over, the one named last changes fastest.
Arguments:
- hidden_frames: bfloat16 [24576, 1280], P('dp', 'fsdp'), may hold values from -6 to 6
- conv_weight: bfloat16 [3, 1280, 1280], P(None, None, 'fsdp'), may hold values from -0.09375 to 0.09375
- conv_bias: bfloat16 [1280], P('fsdp'), may hold values from -4 to 4
- adapter_weight: bfloat16 [1280, 3584], P('fsdp'), may hold values from -0.15625 to 0.15625
- prompt_grad: bfloat16 [12288, 3584], P('dp'), may hold values from -6 to 6
- token_index: int32 [12288], P('dp'), may hold values from 0 to 12287, as said below
- clip_tokens: int32 [32, 6], P('dp'), may hold values from 1 to 256, 384 in all within a row
Outputs:
- grad_hidden: bfloat16 [24576, 1280], P('dp', 'fsdp')
- grad_adapter: float32 [1280, 3584], P('fsdp', 'dp')
- grad_conv: float32 [3, 1280, 1280], P(None, 'dp', 'fsdp')
Inputs may be any that keep to these rules, and one draw needn't show every extreme that they name: `token_index`: each audio token appears exactly once. Token u belongs to index u // 384 of dp. The positions on one index of dp hold at most 24 tokens of any one index of dp, and some pair holds exactly 24. `clip_tokens`: each row sums to 384.
All inputs are finite; a program needn't handle non-finite values.
Results may differ from a plain program's by a relative error of at most 0.0049.
Values may be sent and summed in bfloat16 or wider, within the bound.
A program may use at most 128 MiB of HBM per device.

v0:
```python
import math

import jax
import jax.numpy as jnp
from jax import lax
from jax.sharding import PartitionSpec as P


def gelu_slope(preact):
    return 0.5 * (1.0 + jax.scipy.special.erf(preact / math.sqrt(2.0))) + preact * jnp.exp(
        -0.5 * preact * preact
    ) / math.sqrt(2.0 * math.pi)


def contract_last(left_rows, right_rows):
    return lax.dot_general(
        left_rows, right_rows, (((1,), (1,)), ((), ())), preferred_element_type=jnp.float32
    )


def frame_grads(slope_rows, weights, inside):
    even_part = contract_last(slope_rows, weights[1])
    odd_part = contract_last(slope_rows, weights[2])
    early_part = contract_last(slope_rows, weights[0]) * inside[:, None]
    shifted = jnp.concatenate(
        [early_part[1:], jnp.zeros((1, early_part.shape[1]), jnp.float32)], axis=0
    )
    odd_part = odd_part + shifted
    return jnp.stack([even_part, odd_part], axis=1).reshape(
        2 * slope_rows.shape[0], even_part.shape[1]
    )


def body(
    hidden_frames, conv_weight, conv_bias, adapter_weight, prompt_grad, token_index, clip_tokens
):
    tok_rows = prompt_grad.shape[0]
    dp_count = lax.axis_size("dp")
    slot_cap = 2 * tok_rows // dp_count
    owners = token_index // tok_rows
    local_rows = token_index - owners * tok_rows
    member = (owners[:, None] == jnp.arange(dp_count, dtype=jnp.int32)[None, :]).astype(jnp.int32)
    rank_ids = jnp.sum((jnp.cumsum(member, axis=0) - member) * member, axis=1)
    slot_ids = owners * slot_cap + rank_ids
    send_index = (
        jnp.full((dp_count * slot_cap,), -1, jnp.int32)
        .at[slot_ids]
        .set(local_rows)
        .reshape(dp_count, slot_cap)
    )
    out_width = prompt_grad.shape[1]
    send_rows = (
        jnp.zeros((dp_count * slot_cap, out_width), jnp.bfloat16)
        .at[slot_ids]
        .set(prompt_grad)
        .reshape(dp_count, slot_cap, out_width)
    )
    got_rows, got_index = (
        lax.all_to_all(send_rows, "dp", split_axis=0, concat_axis=0, tiled=True),
        lax.all_to_all(send_index, "dp", split_axis=0, concat_axis=0, tiled=True),
    )
    targets = jnp.where(got_index < 0, tok_rows, got_index).reshape(-1)
    token_grad = (
        jnp.zeros((tok_rows, out_width), jnp.bfloat16)
        .at[targets]
        .set(got_rows.reshape(-1, out_width), mode="drop")
    )
    lengths = clip_tokens[0]
    starts = jnp.cumsum(lengths) - lengths
    inside = jnp.ones((tok_rows,), jnp.float32).at[starts].set(0.0)
    frames = lax.all_gather(hidden_frames, "fsdp", axis=1, tiled=True)
    paired = frames.reshape(tok_rows, 2, frames.shape[1])
    even_frames = paired[:, 0]
    odd_frames = paired[:, 1]
    earlier = jnp.concatenate(
        [jnp.zeros((1, frames.shape[1]), jnp.bfloat16), odd_frames[:-1]], axis=0
    )
    earlier = earlier * inside.astype(jnp.bfloat16)[:, None]
    preact = jnp.dot(earlier, conv_weight[0], preferred_element_type=jnp.float32)
    preact = preact + jnp.dot(even_frames, conv_weight[1], preferred_element_type=jnp.float32)
    preact = preact + jnp.dot(odd_frames, conv_weight[2], preferred_element_type=jnp.float32)
    preact = preact + conv_bias.astype(jnp.float32)[None, :]
    hidden_out = jax.nn.gelu(preact, approximate=False).astype(jnp.bfloat16)
    back_hidden = contract_last(token_grad, adapter_weight)
    slope_rows = (back_hidden * gelu_slope(preact)).astype(jnp.bfloat16)
    grad_scale = 1.0 / math.sqrt(tok_rows * dp_count)
    adapter_part = (
        jnp.dot(hidden_out.T, token_grad, preferred_element_type=jnp.float32) * grad_scale
    )
    conv_part = (
        jnp.stack(
            [
                jnp.dot(source.T, slope_rows, preferred_element_type=jnp.float32)
                for source in (earlier, even_frames, odd_frames)
            ]
        )
        * grad_scale
    )
    grad_adapter, grad_conv = (
        lax.psum_scatter(adapter_part, "dp", scatter_dimension=1, tiled=True),
        lax.psum_scatter(conv_part, "dp", scatter_dimension=1, tiled=True),
    )
    whole_grad = frame_grads(slope_rows, conv_weight, inside)
    grad_hidden = lax.psum_scatter(whole_grad, "fsdp", scatter_dimension=1, tiled=True).astype(
        jnp.bfloat16
    )
    return (grad_hidden, grad_adapter, grad_conv)


def solution(mesh):
    placed = (
        P("dp", "fsdp"),
        P(None, None, "fsdp"),
        P("fsdp"),
        P("fsdp", None),
        P("dp", None),
        P("dp"),
        P("dp", None),
    )
    return jax.shard_map(
        body,
        mesh=mesh,
        in_specs=placed,
        out_specs=(P("dp", "fsdp"), P("fsdp", "dp"), P(None, "dp", "fsdp")),
        check_vma=False,
    )
```

profile of v0, /device:TPU:2, one launch (start us, length us, event | category | flops | bytes accessed | tf_op | source)
XLA Modules:
  0.0 636.0 jit_solution(1736810807214301332)
XLA Ops:
  7.2 0.8 multiply_subtract_fusion
  8.0 0.9 reduce-window.10
  9.2 2.9 scatter_custom_fusion
  12.2 0.7 all_to_all.11
  12.9 11.6 %all-to-all-start = ((s32[32,1,24]{2,1,0:T(1,128)}), s32[32,1,24]{2,1,0:T(1,128)S(1)}, u32[]{:S(2)}, u32[]{:S(2)}) async-start(s32[32,1,24]{2,1,0:T(1,128)} %bitcast.2), calls=%async_computation | async-start | bytes 32768 | tf_op jit(solution)/shard_map/all_to_all | solution.py:60
  24.5 8.9 %scatter_custom_fusion.1 = bf16[768,3584]{1,0:T(8,128)(2,1)} fusion(s32[384]{0:T(512)S(1)} %compare_select_fusion.2, bf16[384,3584]{1,0:T(8,128)(2,1)} %param.11, bf16[]{:T(256)} %constant.40.clone.1), kind=kCustom, calls=%fused_computation.9 | custom fusion | bytes 5505536 | tf_op jit(solution)/shard_map/scatter | solution.py:55
  33.4 10.0 %all-to-all-start.1 = ((bf16[32,24,3584]{2,1,0:T(8,128)(2,1)}), bf16[32,24,3584]{2,1,0:T(8,128)(2,1)}, u32[]{:S(2)}, u32[]{:S(2)}) async-start(bf16[32,24,3584]{2,1,0:T(8,128)(2,1)} %bitcast.84), calls=%async_computation.1 | async-start | bytes 11010048 | tf_op jit(solution)/shard_map/all_to_all | solution.py:59
  43.4 0.7 all-gather.2.cloned.1.call-update
  44.3 0.8 scatter_custom_fusion.3
  45.1 0.5 broadcast.117
  45.6 0.7 reduce.7
  46.5 28.2 %all-gather.2.cloned.1.call-done = bf16[768,1280]{0,1:T(8,128)(2,1)} async-done(((bf16[768,160]{0,1:T(8,128)(2,1)}), bf16[768,1280]{0,1:T(8,128)(2,1)}) %all-gather.2.cloned.1.call-update) | async-done | bytes 1966096 | tf_op jit(solution)/shard_map/all_gather | solution.py:71
  74.7 4.0 copy.18
  78.7 4.1 reshape.102
  82.7 2.1 slice.45
  85.0 0.9 copy-done.6
  85.9 0.6 copy-done.8
  86.5 0.6 fusion.11
  87.0 2.8 fusion.119
  89.9 1.2 copy-done.2
  91.1 0.5 convolution_add_fusion.2
  91.7 0.5 fusion.5
  92.2 71.2 %all-to-all-done.1 = bf16[32,24,3584]{2,1,0:T(8,128)(2,1)} async-done(((bf16[32,24,3584]{2,1,0:T(8,128)(2,1)}), bf16[32,24,3584]{2,1,0:T(8,128)(2,1)}, u32[]{:S(2)}, u32[]{:S(2)}) %all-to-all-start.1) | async-done | bytes 5505056 | tf_op jit(solution)/shard_map/all_to_all | solution.py:59
  163.4 13.7 %scatter_custom_fusion.2 = bf16[384,3584]{1,0:T(8,128)(2,1)} fusion(s32[768]{0:T(1024)S(1)} %fusion.80, bf16[768,3584]{1,0:T(8,128)(2,1)} %bitcast.4, bf16[]{:T(256)} %constant.40.clone.1), kind=kCustom, calls=%fused_computation.16 | custom fusion | bytes 2753024 | tf_op jit(solution)/shard_map/scatter | solution.py:66
  177.1 2.9 fusion.6
  180.0 0.5 convolution_bitcast_fusion.1
  180.9 0.6 copy-done.3
  182.0 1.8 maximum_multiply_fusion
  183.7 5.8 copy.20
  189.6 4.3 convolution_multiply_fusion
  194.0 3.6 copy.25
  197.8 1.1 copy-done.9
  198.9 0.5 convolution_bitcast_fusion
  199.4 0.5 fusion.18
  200.1 0.5 fusion
  200.8 5.0 copy.19
  205.8 5.8 reshape.104
  211.6 5.6 copy.23
  217.2 0.6 copy-done.12
  217.8 0.6 dynamic-slice
  219.1 144.1 %all-reduce.5.cloned.1.call-done = f32[3,1280,160]{2,0,1:T(4,128)} async-done(((f32[3,1280,160]{2,0,1:T(4,128)}), f32[3,1280,160]{2,0,1:T(4,128)}) %all-reduce.5.cloned.1.call-update) | async-done | bytes 2457616
  363.2 0.9 constant_dynamic-slice_fusion
  364.1 0.7 copy.22
  364.8 221.0 %reduce-scatter.9.cloned.1.call-done = f32[112,160]{1,0:T(8,128)} async-done(((f32[3584,160]{1,0:T(8,128)}), f32[112,160]{1,0:T(8,128)}) %reduce-scatter.9.cloned.1.call-update) | async-done | bytes 71696
  585.9 1.6 copy.26
  587.5 39.9 %reduce-scatter.7.cloned.1.call-done = f32[160,768]{1,0:T(8,128)} async-done(((f32[1280,768]{1,0:T(8,128)}), f32[160,768]{1,0:T(8,128)}) %reduce-scatter.7.cloned.1.call-update) | async-done | bytes 491536
  627.4 1.2 copy.24
  628.6 0.8 copy.21
  (46 shorter events, 2.5 us)
Async XLA Ops:
  7.2 169.9 %copy-start = (bf16[160,3584]{1,0:T(8,128)(2,1)S(1)}, bf16[160,3584]{1,0:T(8,128)(2,1)}, u32[]{:S(2)}) copy-start(bf16[160,3584]{1,0:T(8,128)(2,1)} %param.10) | copy-start | bytes 3440644
  12.9 20.5 %all-to-all-start = ((s32[32,1,24]{2,1,0:T(1,128)}), s32[32,1,24]{2,1,0:T(1,128)S(1)}, u32[]{:S(2)}, u32[]{:S(2)}) async-start(s32[32,1,24]{2,1,0:T(1,128)} %bitcast.2), calls=%async_computation | async-start | bytes 32768 | tf_op jit(solution)/shard_map/all_to_all | solution.py:60
  33.4 10.8 %copy-start.10 = (s32[1,6]{1,0:T(1,128)S(1)}, s32[1,6]{1,0:T(1,128)}, u32[]{:S(2)}) copy-start(s32[1,6]{1,0:T(1,128)} %param.13) | copy-start | bytes 76
  33.4 11.8 %copy-start.11 = (bf16[160]{0:T(256)(128)(2,1)S(1)}, bf16[160]{0:T(256)(128)(2,1)}, u32[]{:S(2)}) copy-start(bf16[160]{0:T(256)(128)(2,1)} %param.9) | copy-start | bytes 964
  33.4 130.0 %all-to-all-start.1 = ((bf16[32,24,3584]{2,1,0:T(8,128)(2,1)}), bf16[32,24,3584]{2,1,0:T(8,128)(2,1)}, u32[]{:S(2)}, u32[]{:S(2)}) async-start(bf16[32,24,3584]{2,1,0:T(8,128)(2,1)} %bitcast.84), calls=%async_computation.1 | async-start | bytes 11010048 | tf_op jit(solution)/shard_map/all_to_all | solution.py:59
  43.3 31.4 %all-gather.2.cloned.1.call-start = ((), (), s32[]{:S(2)}) async-start(), calls=%async_computation.4 | async-start | bytes 2211840 | tf_op jit(solution)/shard_map/all_gather | solution.py:71
  44.1 319.1 %all-reduce.5.cloned.1.call-start = ((), (), s32[]{:S(2)}) async-start(), calls=%async_computation.7 | async-start | bytes 10485760
  84.8 1.6 copy-start.8
  85.0 1.0 copy-start.6
  89.8 1.3 copy-start.2
  89.9 1.9 copy-start.4
  177.1 2.9 copy-start.7
  177.1 3.5 copy-start.5
  180.0 1.5 copy-start.3
  189.6 396.3 %reduce-scatter.9.cloned.1.call-start = ((), (), s32[]{:S(2)}) async-start(), calls=%async_computation.6 | async-start | bytes 3784704
  197.6 1.3 copy-start.9
  197.6 429.7 %reduce-scatter.7.cloned.1.call-start = ((), (), s32[]{:S(2)}) async-start(), calls=%async_computation.5 | async-start | bytes 4423680
  217.2 0.7 copy-start.12
  217.2 412.2 %copy-start.1 = (bf16[160,3584]{1,0:T(8,128)(2,1)S(1)}, bf16[160,3584]{1,0:T(8,128)(2,1)}, u32[]{:S(2)}) copy-start(bf16[160,3584]{1,0:T(8,128)(2,1)} %param.10) | copy-start | bytes 3440644
Sparse Core Ops, SparseCore 0:
  46.0 28.6 all-gather.1
  189.7 173.4 all-reduce.4
  367.6 218.2 reduce-scatter.8
  588.3 39.0 reduce-scatter.6
where the time goes:
time: 637 us; the launch traced here: 636 us
  waiting for transfers between devices  505 us (79%)
  local copies, waits for them, and re-layouts  77.9 us (12%)
  starting transfers between devices  21.7 us (3%)
  between operations  14.7 us (2%)
  matrix products  11.4 us (2%)
    unnamed x7, waiting for transfers between devices  406 us
    all_to_all x1, waiting for transfers between devices, body(): lax.all_to_all(send_rows, 'dp', split_axis=0, concat_axis=0, tiled=True)  71.2 us
    all_gather x1, waiting for transfers between devices, body(): frames = lax.all_gather(hidden_frames, 'fsdp', axis=1, tiled=True)  28.2 us
    unnamed x35, local copies, waits for them, and re-layouts  20.5 us
    scatter x1, local copies, waits for them, and re-layouts, body(): token_grad = jnp.zeros((tok_rows, out_width), jnp.bfloat16).at[targets].s...  13.7 us
  transfers between devices with their start and end apart: 6, of which 5 were waited for; matrix products, arithmetic and copies ran while one was open for 9% of the time, Pallas kernels for 0%

commit v1 on v0

v1 whole, which is shorter than its diff:
```python
import math

import jax
import jax.numpy as jnp
from jax import lax
from jax.experimental import pallas as pl
from jax.experimental.pallas import tpu as pltpu
from jax.sharding import PartitionSpec as P

MESH = pl.DeviceIdType.MESH
F32 = jnp.float32
BF16 = jnp.bfloat16

NX, NZ, NY = 4, 8, 4
N_DP, N_FSDP = NX * NZ, 2 * NY
TOK = 384
CH = 160
WIDTH = 3584
CAP = 24
LOW = 128
ECOL, EPAD = WIDTH // N_DP, 128
TAPC = 40
GRAD_SCALE = 1.0 / math.sqrt(TOK * N_DP)


def nn(left, right):
    return lax.dot_general(left, right, (((1,), (0,)), ((), ())), preferred_element_type=F32)


def nt(left, right):
    return lax.dot_general(left, right, (((1,), (1,)), ((), ())), preferred_element_type=F32)


def iota(shape, dim):
    return lax.broadcasted_iota(jnp.int32, shape, dim)


def pick(cond):
    return jnp.where(cond, 1.0, 0.0).astype(F32)


def low_hot(keys):
    rows = iota((N_DP, CAP, TOK), 1)
    return pick(keys[:, None, :] == rows).reshape(N_DP * CAP, TOK).astype(BF16)


def high_hot(keys, group):
    rows = iota((N_DP, 8, TOK), 1)
    hit = (keys[:, None, :] == rows + 6 * group) & (rows < 6)
    return pick(hit).reshape(N_DP * 8, TOK).astype(BF16)


def pack(low_ref, high_ref, rows_t, extra=None):
    low = nt(low_ref[...], rows_t[:LOW])
    tail = rows_t[LOW:]
    zero = jnp.zeros((CH - LOW, TOK), BF16)
    high = extra
    for group in range(4):
        placed = jnp.concatenate([tail if g == group else zero for g in range(4)], axis=0)
        part = nt(high_ref[group], placed)
        high = part if high is None else high + part
    slabs = jnp.concatenate([low.reshape(N_DP, CAP, 128), high.reshape(N_DP, 8, 128)], axis=1)
    return slabs.astype(BF16)


def unpack(low_ref, high_ref, got):
    got = got.astype(F32)
    low = got[:, :CAP, :].reshape(N_DP * CAP, 128).T.astype(BF16)
    high = got[:, CAP:, :].reshape(N_DP * 8, 128).T.astype(BF16)
    low = nn(low, low_ref[...])
    tail = None
    for group in range(4):
        part = nn(high[32 * group : 32 * group + 32], high_ref[group])
        tail = part if tail is None else tail + part
    return jnp.concatenate([low, tail], axis=0)


def kernel(
    frames_ref, weight_ref, bias_ref, adapter_ref, prompt_ref, index_ref, clips_ref,
    hidden_ref, gadapter_ref, gconv_ref,
    prompt_pad, weight_t, weight_in, weight_own, xown, xbuf,
    slow, shigh, dlow, dhigh, send, got, slope_all,
    parts, rs_in, rs_out, zsend, zgot, totals,
    route_ss, route_rs, ag_ss, ag_rs, w_ss, w_rs, rs_ss, rs_rs, z_ss, z_rs,
):
    d = lax.axis_index("dp")
    f = lax.axis_index("fsdp")
    x, z = d // NZ, lax.rem(d, NZ)
    y, c = f // 2, lax.rem(f, 2)
    pending = []

    def at(dp, fs):
        return {"dp": dp, "fsdp": fs}

    def rcopy(src, dst, ssem, rsem, dev):
        return pltpu.make_async_remote_copy(
            src_ref=src, dst_ref=dst, send_sem=ssem, recv_sem=rsem,
            device_id=dev, device_id_type=MESH,
        )

    def go(src, dst, ssem, rsem, dev):
        copy = rcopy(src, dst, ssem, rsem, dev)
        copy.start()
        pending.append(copy)

    def arrived(dst, ssem, rsem):
        rcopy(dst, dst, ssem, rsem, at(d, f)).wait_recv()

    barrier = pltpu.get_barrier_semaphore()

    def greet_dp(k, carry):
        pl.semaphore_signal(
            barrier, inc=1, device_id=at(lax.rem(d + k, N_DP), f), device_id_type=MESH
        )
        return carry

    def greet_fsdp(k, carry):
        pl.semaphore_signal(
            barrier, inc=1, device_id=at(d, lax.rem(f + k, N_FSDP)), device_id_type=MESH
        )
        return carry

    lax.fori_loop(1, N_DP, greet_dp, 0)
    lax.fori_loop(1, N_FSDP, greet_fsdp, 0)

    row = iota((2 * TOK, 2 * TOK), 0)
    col = iota((2 * TOK, 2 * TOK), 1)
    source = jnp.where(row < TOK, 2 * row + 1, 2 * (row - TOK))
    frames_t = nn(pick(col == source).astype(BF16), frames_ref[...]).T
    for q in range(4):
        lines = frames_t[TAPC * q : TAPC * q + TAPC]
        xown[q] = jnp.concatenate([lines[:, :TOK], lines[:, TOK:]], axis=0).astype(BF16)

    pl.semaphore_wait(barrier, N_DP - 1 + N_FSDP - 1)

    yr, yl, yo = lax.rem(y + 1, NY), lax.rem(y + NY - 1, NY), lax.rem(y + 2, NY)

    class Gather:
        def __init__(self, which, own, block, half):
            self.ss, self.rs = ag_ss.at[which], ag_rs.at[which]
            self.own, self.block, self.half = own, block, half

        def send(self, src, dst, k, dev):
            go(src, dst, self.ss.at[k], self.rs.at[k], dev)

        def first(self):
            here = self.block(f)
            self.send(self.own, here, 0, at(d, yr * 2 + c))
            self.send(self.own, here, 1, at(d, yl * 2 + c))
            self.send(self.own, here, 2, at(d, y * 2 + 1 - c))

        def relay(self):
            mate = at(d, y * 2 + 1 - c)
            left, right = yl * 2 + c, yr * 2 + c
            arrived(self.block(left), self.ss.at[0], self.rs.at[0])
            self.send(self.half(left, 0), self.half(left, 0), 3, at(d, yr * 2 + c))
            self.send(self.block(left), self.block(left), 5, mate)
            arrived(self.block(right), self.ss.at[1], self.rs.at[1])
            self.send(self.half(right, 1), self.half(right, 1), 4, at(d, yl * 2 + c))
            self.send(self.block(right), self.block(right), 6, mate)

        def share(self):
            mate = at(d, y * 2 + 1 - c)
            far = yo * 2 + c
            arrived(self.half(far, 0), self.ss.at[3], self.rs.at[3])
            self.send(self.half(far, 0), self.half(far, 0), 7, mate)
            arrived(self.half(far, 1), self.ss.at[4], self.rs.at[4])
            self.send(self.half(far, 1), self.half(far, 1), 8, mate)

        def last(self):
            o = 1 - c
            arrived(self.block(y * 2 + o), self.ss.at[2], self.rs.at[2])
            arrived(self.block(yl * 2 + o), self.ss.at[5], self.rs.at[5])
            arrived(self.block(yr * 2 + o), self.ss.at[6], self.rs.at[6])
            arrived(self.half(yo * 2 + o, 0), self.ss.at[7], self.rs.at[7])
            arrived(self.half(yo * 2 + o, 1), self.ss.at[8], self.rs.at[8])

    frames_ag = Gather(
        0,
        xown,
        lambda g: xbuf.at[pl.ds(4 * g, 4), pl.ds(0, 80), :],
        lambda g, h: xbuf.at[pl.ds(4 * g + 2 * h, 2), pl.ds(0, 80), :],
    )
    frames_ag.first()
    xbuf[pl.ds(4 * f, 4), pl.ds(0, 80), :] = xown[...]

    index = index_ref[...]
    group = iota((N_DP, TOK), 0)
    mine = (index >= group * TOK) & (index < (group + 1) * TOK)
    member = pick(mine)
    before = pick(iota((TOK, TOK), 0) < iota((TOK, TOK), 1)).astype(BF16)
    rank = nn(member.astype(BF16), before)
    local = index - jnp.sum(jnp.where(mine, group, 0), axis=0, keepdims=True) * TOK
    keys = jnp.where(mine, rank.astype(jnp.int32), -1)
    slow[...] = low_hot(keys)
    for g in range(4):
        shigh[g] = high_hot(keys, g)
    own_rank = jnp.max(keys, axis=0, keepdims=True)
    by_rank = pick(iota((128, TOK), 0) == own_rank).astype(BF16)
    part = iota((N_DP, 8, TOK), 1)
    high_bits = jnp.where(mine, (local >> 4) + 1, 0).astype(F32)
    low_bits = jnp.where(mine, local & 15, 0).astype(F32)
    marks = jnp.where(part == 6, high_bits[:, None, :], jnp.where(part == 7, low_bits[:, None, :], 0.0))
    extra = nt(marks.reshape(N_DP * 8, TOK).astype(BF16), by_rank)

    back_t = nt(adapter_ref[...], prompt_ref[...]).astype(BF16)
    send[0] = pack(slow, shigh, back_t, extra)

    def route(which):
        def step(k, carry):
            to = lax.rem(d + k, N_DP)
            rcopy(
                send.at[which, to], got.at[which, d],
                route_ss.at[which, k], route_rs.at[which, k], at(to, f),
            ).start()
            return carry

        lax.fori_loop(1, N_DP, step, 0)
        got[which, pl.ds(d, 1)] = send[which, pl.ds(d, 1)]

    def routed(which):
        def step(k, carry):
            come = lax.rem(d + N_DP - k, N_DP)
            rcopy(
                got.at[which, come], got.at[which, come],
                route_ss.at[which, k], route_rs.at[which, k], at(come, f),
            ).wait_recv()
            return carry

        lax.fori_loop(1, N_DP, step, 0)

    def route_sent(which):
        def step(k, carry):
            to = lax.rem(d + k, N_DP)
            rcopy(
                send.at[which, to], got.at[which, d],
                route_ss.at[which, k], route_rs.at[which, k], at(to, f),
            ).wait_send()
            return carry

        lax.fori_loop(1, N_DP, step, 0)

    route(0)
    frames_ag.relay()

    pad8 = jnp.zeros((8, CH), F32)
    for o in range(N_DP):
        lines = [weight_ref[k, TAPC * o : TAPC * o + TAPC, :].astype(F32) for k in (2, 1, 0)]
        weight_t[:, 128 * o : 128 * o + 128] = jnp.concatenate(lines + [pad8], axis=0).T.astype(BF16)

    frames_ag.share()

    for o in range(N_DP):
        columns = prompt_ref[:, ECOL * o : ECOL * o + ECOL]
        prompt_pad[:, 128 * o : 128 * o + 128] = jnp.concatenate(
            [columns, jnp.zeros((TOK, 128 - ECOL), BF16)], axis=1
        )

    lane = iota((1, TOK), 1)
    inside = jnp.ones((1, TOK), F32)
    start = jnp.int32(0)
    for k in range(6):
        inside = jnp.where(lane == start, 0.0, inside)
        start = start + clips_ref[0, k]

    frames_ag.last()

    def weight_out(k, carry):
        to = lax.rem(f + k, N_FSDP)
        rcopy(
            weight_t.at[:, pl.ds(pl.multiple_of(to * 512, 512), 512)], weight_in.at[f],
            w_ss.at[k], w_rs.at[k], at(d, to),
        ).start()
        return carry

    lax.fori_loop(1, N_FSDP, weight_out, 0)
    weight_in[pl.ds(f, 1)] = weight_t[:, pl.ds(pl.multiple_of(f * 512, 512), 512)][None]

    live = pick(iota((48, TOK), 0) < TAPC) * inside

    def shift_in(o, carry):
        lines = xbuf[pl.ds(o, 1), pl.ds(0, 48), :][0].astype(F32)
        xbuf[pl.ds(o, 1), pl.ds(80, 48), :] = (pltpu.roll(lines, 1, 1) * live).astype(BF16)[None]
        return carry

    lax.fori_loop(0, N_DP, shift_in, 0)

    preact = nn(weight_t[...], xbuf[...].reshape(N_DP * 128, TOK)) + bias_ref[...].astype(F32)
    cumul = 0.5 * (1.0 + lax.erf(preact * (1.0 / math.sqrt(2.0))))
    hidden_t = (preact * cumul).astype(BF16)
    slope = cumul + preact * jnp.exp(-0.5 * preact * preact) * (1.0 / math.sqrt(2.0 * math.pi))

    routed(0)
    tags = got[0, :, CAP:, :].astype(F32)
    numbers = (tags[:, 6, :] - 1.0) * 16.0 + tags[:, 7, :]

    def token_of(rows, first, most):
        spot = iota((N_DP, rows, 128), 1)
        match = (iota((N_DP, rows, 128), 2) == spot + first) & (spot < most)
        picked = jnp.sum(jnp.where(match, numbers[:, None, :], 0.0), axis=2, keepdims=True)
        ok = iota((N_DP, rows, 1), 1) < most
        return jnp.where(ok, picked, -1.0)

    def token_hot(rows, first, most):
        token = iota((N_DP, rows, TOK), 2).astype(F32)
        return pick(token_of(rows, first, most) == token).reshape(N_DP * rows, TOK).astype(BF16)

    dlow[...] = token_hot(CAP, 0, CAP)
    for g in range(4):
        dhigh[g] = token_hot(8, 6 * g, 6)
    send[1] = pack(dlow, dhigh, hidden_t)
    route(1)

    slope_t = (unpack(dlow, dhigh, got[0]) * slope).astype(BF16)
    slope_all[pl.ds(f, 1)] = slope_t[None]
    slope_ag = Gather(
        1,
        slope_all.at[f],
        lambda g: slope_all.at[g],
        lambda g, h: slope_all.at[g, pl.ds(80 * h, 80), :],
    )
    slope_ag.first()

    xr, xl, xo = lax.rem(x + 1, NX), lax.rem(x + NX - 1, NX), lax.rem(x + 2, NX)
    to_right, to_left = at(xr * NZ + z, f), at(xl * NZ + z, f)

    def halves(which, owner, h):
        return parts.at[which, pl.ds(owner * NZ + 4 * h, 4)]

    def rs_send(which, src, k, dev):
        go(src, rs_in.at[which, k], rs_ss.at[which, k], rs_rs.at[which, k], dev)

    def rs_wait(which, k):
        arrived(rs_in.at[which, k], rs_ss.at[which, k], rs_rs.at[which, k])

    def rs_first(which):
        rs_send(which, halves(which, xo, 0), 0, to_right)
        rs_send(which, halves(which, xo, 1), 1, to_left)
        rs_send(which, halves(which, xr, 1), 2, to_right)
        rs_send(which, halves(which, xl, 0), 3, to_left)

    def rs_second(which):
        rs_wait(which, 0)
        rs_out[which, 0] = (halves(which, xr, 0)[...].astype(F32) + rs_in[which, 0].astype(F32)).astype(BF16)
        rs_send(which, rs_out.at[which, 0], 4, to_right)
        rs_wait(which, 1)
        rs_out[which, 1] = (halves(which, xl, 1)[...].astype(F32) + rs_in[which, 1].astype(F32)).astype(BF16)
        rs_send(which, rs_out.at[which, 1], 5, to_left)

    def rs_third(which):
        for k in (2, 3, 4, 5):
            rs_wait(which, k)
        for h, (one, two) in enumerate(((4, 3), (5, 2))):
            total = halves(which, x, h)[...].astype(F32) + rs_in[which, one].astype(F32)
            total = total + rs_in[which, two].astype(F32)
            totals[which, pl.ds(4 * h, 4)] = total
            zsend[which, pl.ds(4 * h, 4)] = total.astype(BF16)

        def step(k, carry):
            to = lax.rem(z + k, NZ)
            rcopy(
                zsend.at[which, to], zgot.at[which, k],
                z_ss.at[which, k], z_rs.at[which, k], at(x * NZ + to, f),
            ).start()
            return carry

        lax.fori_loop(1, NZ, step, 0)

    def rs_last(which):
        total = totals[which, pl.ds(z, 1)][0]
        for k in range(1, NZ):
            arrived(zgot.at[which, k], z_ss.at[which, k], z_rs.at[which, k])
            total = total + zgot[which, k].astype(F32)
        return total * GRAD_SCALE

    def conv_part(o, carry):
        block = xbuf[pl.ds(o, 1)][0]
        parts[0, pl.ds(o, 1)] = nt(slope_all[pl.ds(f, 1)][0], block).astype(BF16)[None]
        return carry

    lax.fori_loop(0, N_DP, conv_part, 0)
    rs_first(0)
    slope_ag.relay()

    routed(1)
    hidden_pos = unpack(slow, shigh, got[1]).astype(BF16)
    for o in range(N_DP):
        parts[1, o] = nn(hidden_pos, prompt_pad[:, 128 * o : 128 * o + 128]).astype(BF16)
    rs_first(1)
    slope_ag.share()
    rs_second(0)

    def weight_come(k, carry):
        come = lax.rem(f + N_FSDP - k, N_FSDP)
        rcopy(
            weight_in.at[come], weight_in.at[come], w_ss.at[k], w_rs.at[k], at(d, come)
        ).wait_recv()
        return carry

    lax.fori_loop(1, N_FSDP, weight_come, 0)
    for g in range(N_FSDP):
        weight_own[:, CH * g : CH * g + CH] = weight_in[g].T
    rs_second(1)
    slope_ag.last()
    grads = nn(weight_own[...], slope_all[...].reshape(N_FSDP * CH, TOK))
    odd, even = [], []
    for q in range(4):
        lines = grads[128 * q : 128 * q + 128]
        odd.append(lines[:TAPC] + pltpu.roll(lines[2 * TAPC : 3 * TAPC] * inside, TOK - 1, 1))
        even.append(lines[TAPC : 2 * TAPC])
    both = jnp.concatenate([jnp.concatenate(odd, axis=0), jnp.concatenate(even, axis=0)], axis=1)
    row = iota((2 * TOK, 2 * TOK), 0)
    col = iota((2 * TOK, 2 * TOK), 1)
    place = jnp.where(col < TOK, 2 * col + 1, 2 * (col - TOK))
    hidden_ref[...] = nt(pick(row == place).astype(BF16), both.astype(BF16)).astype(BF16)

    rs_third(0)
    rs_third(1)
    conv = rs_last(0).T
    gconv_ref[0] = conv[2 * TAPC : 3 * TAPC]
    gconv_ref[1] = conv[TAPC : 2 * TAPC]
    gconv_ref[2] = conv[:TAPC]
    gadapter_ref[...] = rs_last(1)[:, :ECOL]

    for copy in pending:
        copy.wait_send()
    route_sent(0)
    route_sent(1)

    def weight_sent(k, carry):
        to = lax.rem(f + k, N_FSDP)
        rcopy(
            weight_t.at[:, pl.ds(pl.multiple_of(to * 512, 512), 512)], weight_in.at[f],
            w_ss.at[k], w_rs.at[k], at(d, to),
        ).wait_send()
        return carry

    lax.fori_loop(1, N_FSDP, weight_sent, 0)

    def z_sent(k, carry):
        to = lax.rem(z + k, NZ)
        for which in range(2):
            rcopy(
                zsend.at[which, to], zgot.at[which, k],
                z_ss.at[which, k], z_rs.at[which, k], at(x * NZ + to, f),
            ).wait_send()
        return carry

    lax.fori_loop(1, NZ, z_sent, 0)


def body(
    hidden_frames, conv_weight, conv_bias, adapter_weight, prompt_grad, token_index, clip_tokens
):
    vmem = pl.BlockSpec(memory_space=pltpu.VMEM)
    dma = pltpu.SemaphoreType.DMA
    return pl.pallas_call(
        kernel,
        out_shape=(
            jax.ShapeDtypeStruct((2 * TOK, CH), BF16),
            jax.ShapeDtypeStruct((CH, ECOL), F32),
            jax.ShapeDtypeStruct((3, TAPC, CH), F32),
        ),
        in_specs=[vmem] * 6 + [pl.BlockSpec(memory_space=pltpu.SMEM)],
        out_specs=(vmem, vmem, vmem),
        scratch_shapes=[
            pltpu.VMEM((TOK, N_DP * EPAD), BF16),
            pltpu.VMEM((CH, N_DP * 128), BF16),
            pltpu.VMEM((N_FSDP, CH, 512), BF16),
            pltpu.VMEM((512, N_FSDP * CH), BF16),
            pltpu.VMEM((4, 80, TOK), BF16),
            pltpu.VMEM((N_DP, 128, TOK), BF16),
            pltpu.VMEM((N_DP * CAP, TOK), BF16),
            pltpu.VMEM((4, N_DP * 8, TOK), BF16),
            pltpu.VMEM((N_DP * CAP, TOK), BF16),
            pltpu.VMEM((4, N_DP * 8, TOK), BF16),
            pltpu.VMEM((2, N_DP, 32, 128), BF16),
            pltpu.VMEM((2, N_DP, 32, 128), BF16),
            pltpu.VMEM((N_FSDP, CH, TOK), BF16),
            pltpu.VMEM((2, N_DP, CH, 128), BF16),
            pltpu.VMEM((2, 6, 4, CH, 128), BF16),
            pltpu.VMEM((2, 2, 4, CH, 128), BF16),
            pltpu.VMEM((2, NZ, CH, 128), BF16),
            pltpu.VMEM((2, NZ, CH, 128), BF16),
            pltpu.VMEM((2, NZ, CH, 128), F32),
            dma((2, N_DP)), dma((2, N_DP)),
            dma((2, 9)), dma((2, 9)),
            dma((N_FSDP,)), dma((N_FSDP,)),
            dma((2, 6)), dma((2, 6)),
            dma((2, NZ)), dma((2, NZ)),
        ],
        compiler_params=pltpu.CompilerParams(
            collective_id=0, has_side_effects=True, vmem_limit_bytes=56 * 1024 * 1024
        ),
    )(
        hidden_frames,
        conv_weight,
        conv_bias.reshape(CH, 1),
        adapter_weight,
        prompt_grad,
        token_index.reshape(1, TOK),
        clip_tokens,
    )


def solution(mesh):
    placed = (
        P("dp", "fsdp"),
        P(None, None, "fsdp"),
        P("fsdp"),
        P("fsdp", None),
        P("dp", None),
        P("dp"),
        P("dp", None),
    )
    return jax.shard_map(
        body,
        mesh=mesh,
        in_specs=placed,
        out_specs=(P("dp", "fsdp"), P("fsdp", "dp"), P(None, "dp", "fsdp")),
        check_vma=False,
    )
```

time: 637 us -> 92 us (0.14)
  waiting for transfers between devices: 505 us -> 0 us
  Pallas kernels: 0 us -> 78 us
  local copies, waits for them, and re-layouts: 77.9 us -> 13.1 us
  starting transfers between devices: 21.7 us -> 0 us
  between operations: 14.7 us -> 0.64 us
  matrix products: 11.4 us -> 0 us
    unnamed x7 -> x0, waiting for transfers between devices: 406 us -> none
    pallas_call x0 -> x1, Pallas kernels: none -> 78 us  [body(): pl.pallas_call(kernel, out_shape=(jax.ShapeDtypeStruct((2 * TOK, CH), BF1...]
    all_to_all x2 -> x0, waiting for transfers between devices: 71.2 us -> none  [the longest x1 71.2 us: body(): lax.all_to_all(send_rows, 'dp', split_axis=0, concat_axis=0, tiled=True)]
    all_gather x1 -> x0, waiting for transfers between devices: 28.2 us -> none  [body(): frames = lax.all_gather(hidden_frames, 'fsdp', axis=1, tiled=True)]
    scatter x4 -> x0, local copies, waits for them, and re-layouts: 26.2 us -> none  [the longest x1 13.7 us: body(): token_grad = jnp.zeros((tok_rows, out_width), jnp.bfloat16).at[targets].s...]
    all_to_all x2 -> x0, starting transfers between devices: 21.6 us -> none  [the longest x1 11.6 us: body(): lax.all_to_all(send_index, 'dp', split_axis=0, concat_axis=0, tiled=True)]
    unnamed x35 -> x4, local copies, waits for them, and re-layouts: 20.5 us -> 8.61 us
    dot_general x11 -> x0, matrix products: 11.4 us -> none  [the longest x1 4.34 us: body(): jnp.dot(hidden_out.T, token_grad, preferred_element_type=jnp.float32)]
  transfers between devices with their start and end apart: 6 -> 0, of which waited for: 5 -> 0; matrix products, arithmetic and copies ran while one was open for 9% -> 0% of each run, Pallas kernels for 0% -> 0%
where the time goes in v1:
time: 92 us; the launch traced here: 91.7 us
  Pallas kernels  78 us (85%)
  local copies, waits for them, and re-layouts  13.1 us (14%)
    pallas_call x1, Pallas kernels, body(): pl.pallas_call(kernel, out_shape=(jax.ShapeDtypeStruct((2 * TOK, CH), BF1...  78 us
    unnamed x4, local copies, waits for them, and re-layouts  8.61 us

profile of v1, /device:TPU:2, one launch (start us, length us, event | category | flops | bytes accessed | tf_op | source)
XLA Modules:
  0.0 91.7 jit_solution(11371586219319186617)
XLA Ops:
  0.6 1.2 %reshape.13.index_ref = s32[1,384]{1,0:T(1,128)} reshape(s32[384]{0:T(512)} %param.12) | data formatting | bytes 3072 | tf_op jit(solution)/shard_map/reshape | solution.py:501
  1.9 1.4 %reshape.14.bias_ref = bf16[160,1]{1,0:T(8,128)(2,1)} reshape(bf16[160]{0:T(256)(128)(2,1)} %param.9) | data formatting | bytes 640 | tf_op jit(solution)/shard_map/reshape | solution.py:498
  3.2 1.9 %copy.13.frames_ref = bf16[768,160]{1,0:T(8,128)(2,1)} copy(bf16[768,160]{0,1:T(8,128)(2,1)} %param.7) | data formatting | bytes 491520 | tf_op args[0]
  5.1 3.6 %copy.14.weight_ref = bf16[3,1280,160]{2,1,0:T(8,128)(2,1)} copy(bf16[3,1280,160]{1,2,0:T(8,128)(2,1)} %param.8) | data formatting | bytes 2457600 | tf_op args[1]
  8.8 78.0 %shard_map.94 = (bf16[768,160]{1,0:T(8,128)(2,1)}, f32[160,112]{1,0:T(8,128)}, f32[3,40,160]{2,1,0:T(8,128)}) custom-call(bf16[768,160]{1,0:T(8,128)(2,1)} %copy.13.frames_ref, bf16[3,1280,160]{2,1,0:T(8,128)(2,1)} %copy.14.weight_ref, bf16[160,1]{1,0:T(8,128)(2,1)} %reshape.14.bias_ref, bf16[160,3584]{1,0:T(8,128)(2,1)} %adapter_ref.1, ...), custom_call_target="tpu_custom_call" | custom-call | tf_op jit(solution)/shard_map/pallas_call | solution.py:457
  86.7 1.8 %copy.16 = bf16[768,160]{0,1:T(8,128)(2,1)} copy(bf16[768,160]{1,0:T(8,128)(2,1)} %get-tuple-element.6) | data formatting | bytes 491520 | tf_op jit(solution)/shard_map/pallas_call | solution.py:457
  88.6 1.5 %copy.19 = f32[160,112]{1,0:T(8,128)} copy(f32[160,112]{1,0:T(8,128)} %get-tuple-element.13) | data formatting | bytes 143360
  90.1 1.6 %copy.20 = f32[3,40,160]{2,1,0:T(8,128)} copy(f32[3,40,160]{2,1,0:T(8,128)} %get-tuple-element.14) | data formatting | bytes 153600

commit v2 on v1

--- a/solution.py
+++ b/solution.py
@@ -76,8 +76,9 @@
 
 
 def kernel(
-    frames_ref, weight_ref, bias_ref, adapter_ref, prompt_ref, index_ref, clips_ref,
-    hidden_ref, gadapter_ref, gconv_ref,
+    frames_hbm, weight_hbm, bias_ref, adapter_hbm, prompt_hbm, index_ref, clips_ref,
+    hidden_ref, sums_ref,
+    frames_ref, weight_ref, adapter_ref, prompt_ref, in_sem, halving,
     prompt_pad, weight_t, weight_in, weight_own, xown, xbuf,
     slow, shigh, dlow, dhigh, send, got, slope_all,
     parts, rs_in, rs_out, zsend, zgot, totals,
@@ -88,6 +89,19 @@
     x, z = d // NZ, lax.rem(d, NZ)
     y, c = f // 2, lax.rem(f, 2)
     pending = []
+    loads = [
+        pltpu.make_async_copy(src, dst, in_sem.at[k])
+        for k, (src, dst) in enumerate(
+            (
+                (frames_hbm, frames_ref),
+                (adapter_hbm, adapter_ref),
+                (prompt_hbm, prompt_ref),
+                (weight_hbm, weight_ref),
+            )
+        )
+    ]
+    for load in loads:
+        load.start()
 
     def at(dp, fs):
         return {"dp": dp, "fsdp": fs}
@@ -123,13 +137,17 @@
     lax.fori_loop(1, N_DP, greet_dp, 0)
     lax.fori_loop(1, N_FSDP, greet_fsdp, 0)
 
-    row = iota((2 * TOK, 2 * TOK), 0)
-    col = iota((2 * TOK, 2 * TOK), 1)
-    source = jnp.where(row < TOK, 2 * row + 1, 2 * (row - TOK))
-    frames_t = nn(pick(col == source).astype(BF16), frames_ref[...]).T
-    for q in range(4):
-        lines = frames_t[TAPC * q : TAPC * q + TAPC]
-        xown[q] = jnp.concatenate([lines[:, :TOK], lines[:, TOK:]], axis=0).astype(BF16)
+    row = iota((256, 256), 0)
+    col = iota((256, 256), 1)
+    halving[...] = pick(row == jnp.where(col < 128, 2 * col + 1, 2 * (col - 128))).astype(BF16)
+    loads[0].wait()
+    for b in range(3):
+        lines = nn(frames_ref[:, 256 * b : 256 * b + 256], halving[...])
+        for q in range(4):
+            quarter = lines[TAPC * q : TAPC * q + TAPC]
+            xown[q, :, 128 * b : 128 * b + 128] = jnp.concatenate(
+                [quarter[:, :128], quarter[:, 128:]], axis=0
+            ).astype(BF16)
 
     pl.semaphore_wait(barrier, N_DP - 1 + N_FSDP - 1)
 
@@ -184,7 +202,7 @@
     frames_ag.first()
     xbuf[pl.ds(4 * f, 4), pl.ds(0, 80), :] = xown[...]
 
-    index = index_ref[...]
+    index = index_ref[...].reshape(1, TOK)
     group = iota((N_DP, TOK), 0)
     mine = (index >= group * TOK) & (index < (group + 1) * TOK)
     member = pick(mine)
@@ -203,6 +221,8 @@
     marks = jnp.where(part == 6, high_bits[:, None, :], jnp.where(part == 7, low_bits[:, None, :], 0.0))
     extra = nt(marks.reshape(N_DP * 8, TOK).astype(BF16), by_rank)
 
+    loads[1].wait()
+    loads[2].wait()
     back_t = nt(adapter_ref[...], prompt_ref[...]).astype(BF16)
     send[0] = pack(slow, shigh, back_t, extra)
 
@@ -243,10 +263,11 @@
     route(0)
     frames_ag.relay()
 
-    pad8 = jnp.zeros((8, CH), F32)
+    loads[3].wait()
+    pad8 = jnp.zeros((CH, 8), BF16)
     for o in range(N_DP):
-        lines = [weight_ref[k, TAPC * o : TAPC * o + TAPC, :].astype(F32) for k in (2, 1, 0)]
-        weight_t[:, 128 * o : 128 * o + 128] = jnp.concatenate(lines + [pad8], axis=0).T.astype(BF16)
+        lines = [weight_ref[k, :, TAPC * o : TAPC * o + TAPC] for k in (2, 1, 0)]
+        weight_t[:, 128 * o : 128 * o + 128] = jnp.concatenate(lines + [pad8], axis=1)
 
     frames_ag.share()
 
@@ -285,7 +306,9 @@
 
     lax.fori_loop(0, N_DP, shift_in, 0)
 
-    preact = nn(weight_t[...], xbuf[...].reshape(N_DP * 128, TOK)) + bias_ref[...].astype(F32)
+    bias = bias_ref[...].astype(F32).reshape(1, CH)
+    bias = jnp.sum(jnp.where(iota((CH, CH), 0) == iota((CH, CH), 1), bias, 0.0), axis=1, keepdims=True)
+    preact = nn(weight_t[...], xbuf[...].reshape(N_DP * 128, TOK)) + bias
     cumul = 0.5 * (1.0 + lax.erf(preact * (1.0 / math.sqrt(2.0))))
     hidden_t = (preact * cumul).astype(BF16)
     slope = cumul + preact * jnp.exp(-0.5 * preact * preact) * (1.0 / math.sqrt(2.0 * math.pi))
@@ -408,19 +431,18 @@
         lines = grads[128 * q : 128 * q + 128]
         odd.append(lines[:TAPC] + pltpu.roll(lines[2 * TAPC : 3 * TAPC] * inside, TOK - 1, 1))
         even.append(lines[TAPC : 2 * TAPC])
-    both = jnp.concatenate([jnp.concatenate(odd, axis=0), jnp.concatenate(even, axis=0)], axis=1)
-    row = iota((2 * TOK, 2 * TOK), 0)
-    col = iota((2 * TOK, 2 * TOK), 1)
-    place = jnp.where(col < TOK, 2 * col + 1, 2 * (col - TOK))
-    hidden_ref[...] = nt(pick(row == place).astype(BF16), both.astype(BF16)).astype(BF16)
+    odd = jnp.concatenate(odd, axis=0).astype(BF16)
+    even = jnp.concatenate(even, axis=0).astype(BF16)
+    for b in range(3):
+        both = jnp.concatenate(
+            [odd[:, 128 * b : 128 * b + 128], even[:, 128 * b : 128 * b + 128]], axis=1
+        )
+        hidden_ref[:, 256 * b : 256 * b + 256] = nt(both, halving[...]).astype(BF16)
 
     rs_third(0)
     rs_third(1)
-    conv = rs_last(0).T
-    gconv_ref[0] = conv[2 * TAPC : 3 * TAPC]
-    gconv_ref[1] = conv[TAPC : 2 * TAPC]
-    gconv_ref[2] = conv[:TAPC]
-    gadapter_ref[...] = rs_last(1)[:, :ECOL]
+    sums_ref[0] = rs_last(0)
+    sums_ref[1] = rs_last(1)
 
     for copy in pending:
         copy.wait_send()
@@ -449,21 +471,37 @@
     lax.fori_loop(1, NZ, z_sent, 0)
 
 
+def finish(hidden_in, sums_ref, hidden_ref, gadapter_ref, gconv_ref):
+    hidden_ref[...] = hidden_in[...]
+    conv = sums_ref[0].T
+    gconv_ref[0] = conv[2 * TAPC : 3 * TAPC]
+    gconv_ref[1] = conv[TAPC : 2 * TAPC]
+    gconv_ref[2] = conv[:TAPC]
+    gadapter_ref[...] = sums_ref[1][:, :ECOL]
+
+
 def body(
     hidden_frames, conv_weight, conv_bias, adapter_weight, prompt_grad, token_index, clip_tokens
 ):
     vmem = pl.BlockSpec(memory_space=pltpu.VMEM)
+    smem = pl.BlockSpec(memory_space=pltpu.SMEM)
+    hbm = pl.BlockSpec(memory_space=pl.ANY)
     dma = pltpu.SemaphoreType.DMA
-    return pl.pallas_call(
+    hidden, sums = pl.pallas_call(
         kernel,
         out_shape=(
-            jax.ShapeDtypeStruct((2 * TOK, CH), BF16),
-            jax.ShapeDtypeStruct((CH, ECOL), F32),
-            jax.ShapeDtypeStruct((3, TAPC, CH), F32),
+            jax.ShapeDtypeStruct((CH, 2 * TOK), BF16),
+            jax.ShapeDtypeStruct((2, CH, 128), F32),
         ),
-        in_specs=[vmem] * 6 + [pl.BlockSpec(memory_space=pltpu.SMEM)],
-        out_specs=(vmem, vmem, vmem),
+        in_specs=[hbm, hbm, vmem, hbm, hbm, vmem, smem],
+        out_specs=(vmem, vmem),
         scratch_shapes=[
+            pltpu.VMEM((CH, 2 * TOK), BF16),
+            pltpu.VMEM((3, CH, N_FSDP * CH), BF16),
+            pltpu.VMEM((CH, WIDTH), BF16),
+            pltpu.VMEM((TOK, WIDTH), BF16),
+            dma((4,)),
+            pltpu.VMEM((256, 256), BF16),
             pltpu.VMEM((TOK, N_DP * EPAD), BF16),
             pltpu.VMEM((CH, N_DP * 128), BF16),
             pltpu.VMEM((N_FSDP, CH, 512), BF16),
@@ -493,14 +531,25 @@
             collective_id=0, has_side_effects=True, vmem_limit_bytes=56 * 1024 * 1024
         ),
     )(
-        hidden_frames,
-        conv_weight,
-        conv_bias.reshape(CH, 1),
+        hidden_frames.T,
+        jnp.swapaxes(conv_weight, 1, 2),
+        conv_bias,
         adapter_weight,
         prompt_grad,
-        token_index.reshape(1, TOK),
+        token_index,
         clip_tokens,
     )
+    hidden, gadapter, gconv = pl.pallas_call(
+        finish,
+        out_shape=(
+            jax.ShapeDtypeStruct((CH, 2 * TOK), BF16),
+            jax.ShapeDtypeStruct((CH, ECOL), F32),
+            jax.ShapeDtypeStruct((3, TAPC, CH), F32),
+        ),
+        in_specs=[vmem, vmem],
+        out_specs=(vmem, vmem, vmem),
+    )(hidden, sums)
+    return (hidden.T, gadapter, gconv)
 
 
 def solution(mesh):

time: 92 us -> 78.6 us (0.85)
  local copies, waits for them, and re-layouts: 13.1 us -> 0 us
    unnamed x4 -> x0, local copies, waits for them, and re-layouts: 8.61 us -> none
    reshape x2 -> x0, local copies, waits for them, and re-layouts: 2.61 us -> none  [the longest x1 1.36 us: body(): conv_bias.reshape(CH, 1)]
    pallas_call x1 -> x0, local copies, waits for them, and re-layouts: 1.84 us -> none  [body(): pl.pallas_call(kernel, out_shape=(jax.ShapeDtypeStruct((2 * TOK, CH), BF1...]
    pallas_call x1 -> x2, Pallas kernels: 78 us -> 77.8 us  [the longest x1 76 us: body(): pl.pallas_call(kernel, out_shape=(jax.ShapeDtypeStruct((CH, 2 * TOK), BF1...]
where the time goes in v2:
time: 78.6 us; the launch traced here: 78.5 us
  Pallas kernels  77.8 us (99%)
    pallas_call x1, Pallas kernels, body(): pl.pallas_call(kernel, out_shape=(jax.ShapeDtypeStruct((CH, 2 * TOK), BF1...  76 us
    pallas_call x1, Pallas kernels, body(): pl.pallas_call(finish, out_shape=(jax.ShapeDtypeStruct((CH, 2 * TOK), BF1...  1.81 us

profile of v2, /device:TPU:2, one launch (start us, length us, event | category | flops | bytes accessed | tf_op | source)
XLA Modules:
  0.0 78.5 jit_solution(13075325578638762508)
XLA Ops:
  0.6 76.0 %shard_map.94 = (bf16[160,768]{1,0:T(8,128)(2,1)}, f32[2,160,128]{2,1,0:T(8,128)}) custom-call(bf16[160,768]{1,0:T(8,128)(2,1)} %bitcast.4, bf16[3,160,1280]{2,1,0:T(8,128)(2,1)} %bitcast.3, bf16[160]{0:T(256)(128)(2,1)} %bias_ref.1, bf16[160,3584]{1,0:T(8,128)(2,1)} %adapter_hbm.1, bf16[384,3584]{1,0:T(8,128)(2,1)} %prompt_hbm.1, s32[384]{0:T(512)} %index_ref.1, ...), custom_call_target="tpu_custom_call" | custom-call | tf_op jit(solution)/shard_map/pallas_call | solution.py:490
  76.7 1.8 %shard_map.95 = (bf16[160,768]{1,0:T(8,128)(2,1)}, f32[160,112]{1,0:T(8,128)}, f32[3,40,160]{2,1,0:T(8,128)}) custom-call(bf16[160,768]{1,0:T(8,128)(2,1)} %get-tuple-element.8.hidden_in, f32[2,160,128]{2,1,0:T(8,128)} %get-tuple-element.9.sums_ref), custom_call_target="tpu_custom_call" | custom-call | tf_op jit(solution)/shard_map/pallas_call | solution.py:542

commit v3 on v2

--- a/solution.py
+++ b/solution.py
@@ -79,7 +79,7 @@
     frames_hbm, weight_hbm, bias_ref, adapter_hbm, prompt_hbm, index_ref, clips_ref,
     hidden_ref, sums_ref,
     frames_ref, weight_ref, adapter_ref, prompt_ref, in_sem, halving,
-    prompt_pad, weight_t, weight_in, weight_own, xown, xbuf,
+    preact_ref, back_ref, prompt_pad, weight_t, weight_in, weight_own, xown, xbuf,
     slow, shigh, dlow, dhigh, send, got, slope_all,
     parts, rs_in, rs_out, zsend, zgot, totals,
     route_ss, route_rs, ag_ss, ag_rs, w_ss, w_rs, rs_ss, rs_rs, z_ss, z_rs,
@@ -152,53 +152,33 @@
     pl.semaphore_wait(barrier, N_DP - 1 + N_FSDP - 1)
 
     yr, yl, yo = lax.rem(y + 1, NY), lax.rem(y + NY - 1, NY), lax.rem(y + 2, NY)
+    mate = at(d, y * 2 + 1 - c)
 
     class Gather:
-        def __init__(self, which, own, block, half):
+        def __init__(self, which, own, block):
             self.ss, self.rs = ag_ss.at[which], ag_rs.at[which]
-            self.own, self.block, self.half = own, block, half
+            self.own, self.block = own, block
+            self.order = (yl, yr, yo)
 
         def send(self, src, dst, k, dev):
             go(src, dst, self.ss.at[k], self.rs.at[k], dev)
 
         def first(self):
             here = self.block(f)
-            self.send(self.own, here, 0, at(d, yr * 2 + c))
-            self.send(self.own, here, 1, at(d, yl * 2 + c))
-            self.send(self.own, here, 2, at(d, y * 2 + 1 - c))
-
-        def relay(self):
-            mate = at(d, y * 2 + 1 - c)
-            left, right = yl * 2 + c, yr * 2 + c
-            arrived(self.block(left), self.ss.at[0], self.rs.at[0])
-            self.send(self.half(left, 0), self.half(left, 0), 3, at(d, yr * 2 + c))
-            self.send(self.block(left), self.block(left), 5, mate)
-            arrived(self.block(right), self.ss.at[1], self.rs.at[1])
-            self.send(self.half(right, 1), self.half(right, 1), 4, at(d, yl * 2 + c))
-            self.send(self.block(right), self.block(right), 6, mate)
-
-        def share(self):
-            mate = at(d, y * 2 + 1 - c)
-            far = yo * 2 + c
-            arrived(self.half(far, 0), self.ss.at[3], self.rs.at[3])
-            self.send(self.half(far, 0), self.half(far, 0), 7, mate)
-            arrived(self.half(far, 1), self.ss.at[4], self.rs.at[4])
-            self.send(self.half(far, 1), self.half(far, 1), 8, mate)
-
-        def last(self):
-            o = 1 - c
-            arrived(self.block(y * 2 + o), self.ss.at[2], self.rs.at[2])
-            arrived(self.block(yl * 2 + o), self.ss.at[5], self.rs.at[5])
-            arrived(self.block(yr * 2 + o), self.ss.at[6], self.rs.at[6])
-            arrived(self.half(yo * 2 + o, 0), self.ss.at[7], self.rs.at[7])
-            arrived(self.half(yo * 2 + o, 1), self.ss.at[8], self.rs.at[8])
-
-    frames_ag = Gather(
-        0,
-        xown,
-        lambda g: xbuf.at[pl.ds(4 * g, 4), pl.ds(0, 80), :],
-        lambda g, h: xbuf.at[pl.ds(4 * g + 2 * h, 2), pl.ds(0, 80), :],
-    )
+            for k, to in enumerate((yr, yl, yo)):
+                self.send(self.own, here, k, at(d, to * 2 + c))
+            self.send(self.own, here, 3, mate)
+
+        def forward(self, k):
+            block = self.block(self.order[k] * 2 + c)
+            arrived(block, self.ss.at[k], self.rs.at[k])
+            self.send(block, block, 4 + k, mate)
+
+        def from_mate(self, k):
+            come = y if k == 3 else self.order[k - 4]
+            arrived(self.block(come * 2 + 1 - c), self.ss.at[k], self.rs.at[k])
+
+    frames_ag = Gather(0, xown, lambda g: xbuf.at[pl.ds(4 * g, 4), pl.ds(0, 80), :])
     frames_ag.first()
     xbuf[pl.ds(4 * f, 4), pl.ds(0, 80), :] = xown[...]
 
@@ -261,21 +241,12 @@
         lax.fori_loop(1, N_DP, step, 0)
 
     route(0)
-    frames_ag.relay()
 
     loads[3].wait()
     pad8 = jnp.zeros((CH, 8), BF16)
     for o in range(N_DP):
         lines = [weight_ref[k, :, TAPC * o : TAPC * o + TAPC] for k in (2, 1, 0)]
         weight_t[:, 128 * o : 128 * o + 128] = jnp.concatenate(lines + [pad8], axis=1)
-
-    frames_ag.share()
-
-    for o in range(N_DP):
-        columns = prompt_ref[:, ECOL * o : ECOL * o + ECOL]
-        prompt_pad[:, 128 * o : 128 * o + 128] = jnp.concatenate(
-            [columns, jnp.zeros((TOK, 128 - ECOL), BF16)], axis=1
-        )
 
     lane = iota((1, TOK), 1)
     inside = jnp.ones((1, TOK), F32)
@@ -283,8 +254,33 @@
     for k in range(6):
         inside = jnp.where(lane == start, 0.0, inside)
         start = start + clips_ref[0, k]
-
-    frames_ag.last()
+    live = pick(iota((48, TOK), 0) < TAPC) * inside
+
+    bias = bias_ref[...].astype(F32).reshape(1, CH)
+    bias = jnp.sum(jnp.where(iota((CH, CH), 0) == iota((CH, CH), 1), bias, 0.0), axis=1, keepdims=True)
+    preact_ref[...] = jnp.broadcast_to(bias, (CH, TOK))
+
+    def preact_block(g):
+        for q in range(4):
+            lines = xbuf[pl.ds(4 * g + q, 1), pl.ds(0, 48), :][0].astype(F32)
+            early = (pltpu.roll(lines, 1, 1) * live).astype(BF16)
+            xbuf[pl.ds(4 * g + q, 1), pl.ds(80, 48), :] = early[None]
+        block = xbuf[pl.ds(4 * g, 4)].reshape(512, TOK)
+        preact_ref[...] += nn(weight_t[:, pl.ds(pl.multiple_of(g * 512, 512), 512)], block)
+
+    preact_block(f)
+    for k in range(2):
+        frames_ag.forward(k)
+    frames_ag.from_mate(3)
+    preact_block(y * 2 + 1 - c)
+
+    for o in range(N_DP // 2):
+        columns = prompt_ref[:, ECOL * o : ECOL * o + ECOL]
+        prompt_pad[:, 128 * o : 128 * o + 128] = jnp.concatenate(
+            [columns, jnp.zeros((TOK, 128 - ECOL), BF16)], axis=1
+        )
+
+    frames_ag.forward(2)
 
     def weight_out(k, carry):
         to = lax.rem(f + k, N_FSDP)
@@ -297,21 +293,8 @@
     lax.fori_loop(1, N_FSDP, weight_out, 0)
     weight_in[pl.ds(f, 1)] = weight_t[:, pl.ds(pl.multiple_of(f * 512, 512), 512)][None]
 
-    live = pick(iota((48, TOK), 0) < TAPC) * inside
-
-    def shift_in(o, carry):
-        lines = xbuf[pl.ds(o, 1), pl.ds(0, 48), :][0].astype(F32)
-        xbuf[pl.ds(o, 1), pl.ds(80, 48), :] = (pltpu.roll(lines, 1, 1) * live).astype(BF16)[None]
-        return carry
-
-    lax.fori_loop(0, N_DP, shift_in, 0)
-
-    bias = bias_ref[...].astype(F32).reshape(1, CH)
-    bias = jnp.sum(jnp.where(iota((CH, CH), 0) == iota((CH, CH), 1), bias, 0.0), axis=1, keepdims=True)
-    preact = nn(weight_t[...], xbuf[...].reshape(N_DP * 128, TOK)) + bias
-    cumul = 0.5 * (1.0 + lax.erf(preact * (1.0 / math.sqrt(2.0))))
-    hidden_t = (preact * cumul).astype(BF16)
-    slope = cumul + preact * jnp.exp(-0.5 * preact * preact) * (1.0 / math.sqrt(2.0 * math.pi))
+    for k in range(3):
+        preact_block(frames_ag.order[k] * 2 + c)
 
     routed(0)
     tags = got[0, :, CAP:, :].astype(F32)
@@ -331,17 +314,22 @@
     dlow[...] = token_hot(CAP, 0, CAP)
     for g in range(4):
         dhigh[g] = token_hot(8, 6 * g, 6)
+    back_ref[...] = unpack(dlow, dhigh, got[0])
+
+    for k in range(3):
+        frames_ag.from_mate(4 + k)
+        preact_block(frames_ag.order[k] * 2 + 1 - c)
+
+    preact = preact_ref[...]
+    cumul = 0.5 * (1.0 + lax.erf(preact * (1.0 / math.sqrt(2.0))))
+    hidden_t = (preact * cumul).astype(BF16)
     send[1] = pack(dlow, dhigh, hidden_t)
     route(1)
 
-    slope_t = (unpack(dlow, dhigh, got[0]) * slope).astype(BF16)
+    slope = cumul + preact * jnp.exp(-0.5 * preact * preact) * (1.0 / math.sqrt(2.0 * math.pi))
+    slope_t = (back_ref[...] * slope).astype(BF16)
     slope_all[pl.ds(f, 1)] = slope_t[None]
-    slope_ag = Gather(
-        1,
-        slope_all.at[f],
-        lambda g: slope_all.at[g],
-        lambda g, h: slope_all.at[g, pl.ds(80 * h, 80), :],
-    )
+    slope_ag = Gather(1, slope_all.at[f], lambda g: slope_all.at[g])
     slope_ag.first()
 
     xr, xl, xo = lax.rem(x + 1, NX), lax.rem(x + NX - 1, NX), lax.rem(x + 2, NX)
@@ -356,11 +344,17 @@
     def rs_wait(which, k):
         arrived(rs_in.at[which, k], rs_ss.at[which, k], rs_rs.at[which, k])
 
-    def rs_first(which):
+    def rs_first(which, part):
+        part(xo, 0)
         rs_send(which, halves(which, xo, 0), 0, to_right)
+        part(xo, 1)
         rs_send(which, halves(which, xo, 1), 1, to_left)
+        part(xr, 1)
         rs_send(which, halves(which, xr, 1), 2, to_right)
+        part(xl, 0)
         rs_send(which, halves(which, xl, 0), 3, to_left)
+        part(xr, 0)
+        part(xl, 1)
 
     def rs_second(which):
         rs_wait(which, 0)
@@ -396,22 +390,37 @@
             total = total + zgot[which, k].astype(F32)
         return total * GRAD_SCALE
 
-    def conv_part(o, carry):
-        block = xbuf[pl.ds(o, 1)][0]
-        parts[0, pl.ds(o, 1)] = nt(slope_all[pl.ds(f, 1)][0], block).astype(BF16)[None]
-        return carry
-
-    lax.fori_loop(0, N_DP, conv_part, 0)
-    rs_first(0)
-    slope_ag.relay()
+    def store_parts(which, g, block):
+        for q in range(4):
+            parts[which, pl.ds(4 * g + q, 1)] = block[:, 128 * q : 128 * q + 128].astype(BF16)[None]
+
+    def conv_part(owner, h):
+        g = 2 * owner + h
+        store_parts(0, g, nt(slope_t, xbuf[pl.ds(4 * g, 4)].reshape(512, TOK)))
+
+    def adapter_part(owner, h):
+        g = 2 * owner + h
+        store_parts(1, g, nn(hidden_pos, prompt_pad[:, pl.ds(pl.multiple_of(g * 512, 512), 512)]))
+
+    rs_first(0, conv_part)
+    for o in range(N_DP // 2, N_DP):
+        columns = prompt_ref[:, ECOL * o : ECOL * o + ECOL]
+        prompt_pad[:, 128 * o : 128 * o + 128] = jnp.concatenate(
+            [columns, jnp.zeros((TOK, 128 - ECOL), BF16)], axis=1
+        )
+    conv_part(x, 0)
+    conv_part(x, 1)
 
     routed(1)
     hidden_pos = unpack(slow, shigh, got[1]).astype(BF16)
-    for o in range(N_DP):
-        parts[1, o] = nn(hidden_pos, prompt_pad[:, 128 * o : 128 * o + 128]).astype(BF16)
-    rs_first(1)
-    slope_ag.share()
+    rs_first(1, adapter_part)
     rs_second(0)
+    for k in range(3):
+        slope_ag.forward(k)
+    adapter_part(x, 0)
+    adapter_part(x, 1)
+    rs_third(0)
+    rs_second(1)
 
     def weight_come(k, carry):
         come = lax.rem(f + N_FSDP - k, N_FSDP)
@@ -423,8 +432,10 @@
     lax.fori_loop(1, N_FSDP, weight_come, 0)
     for g in range(N_FSDP):
         weight_own[:, CH * g : CH * g + CH] = weight_in[g].T
-    rs_second(1)
-    slope_ag.last()
+    rs_third(1)
+
+    for k in range(3, 7):
+        slope_ag.from_mate(k)
     grads = nn(weight_own[...], slope_all[...].reshape(N_FSDP * CH, TOK))
     odd, even = [], []
     for q in range(4):
@@ -439,8 +450,6 @@
         )
         hidden_ref[:, 256 * b : 256 * b + 256] = nt(both, halving[...]).astype(BF16)
 
-    rs_third(0)
-    rs_third(1)
     sums_ref[0] = rs_last(0)
     sums_ref[1] = rs_last(1)
 
@@ -502,6 +511,8 @@
             pltpu.VMEM((TOK, WIDTH), BF16),
             dma((4,)),
             pltpu.VMEM((256, 256), BF16),
+            pltpu.VMEM((CH, TOK), F32),
+            pltpu.VMEM((CH, TOK), F32),
             pltpu.VMEM((TOK, N_DP * EPAD), BF16),
             pltpu.VMEM((CH, N_DP * 128), BF16),
             pltpu.VMEM((N_FSDP, CH, 512), BF16),
@@ -522,7 +533,7 @@
             pltpu.VMEM((2, NZ, CH, 128), BF16),
             pltpu.VMEM((2, NZ, CH, 128), F32),
             dma((2, N_DP)), dma((2, N_DP)),
-            dma((2, 9)), dma((2, 9)),
+            dma((2, 7)), dma((2, 7)),
             dma((N_FSDP,)), dma((N_FSDP,)),
             dma((2, 6)), dma((2, 6)),
             dma((2, NZ)), dma((2, NZ)),

time: 78.6 us -> 72.4 us (0.921); the launches traced: 78.5 us -> 71.4 us
  Pallas kernels: 77.8 us -> 70.8 us
    pallas_call x1, Pallas kernels: 76 us -> 69 us  [body(): pl.pallas_call(kernel, out_shape=(jax.ShapeDtypeStruct((CH, 2 * TOK), BF1...]
where the time goes in v3:
time: 72.4 us; the launch traced here: 71.4 us
  Pallas kernels  70.8 us (98%)
    pallas_call x1, Pallas kernels, body(): pl.pallas_call(kernel, out_shape=(jax.ShapeDtypeStruct((CH, 2 * TOK), BF1...  69 us
    pallas_call x1, Pallas kernels, body(): pl.pallas_call(finish, out_shape=(jax.ShapeDtypeStruct((CH, 2 * TOK), BF1...  1.81 us

profile of v3, /device:TPU:2, one launch (start us, length us, event | category | flops | bytes accessed | tf_op | source)
XLA Modules:
  0.0 71.4 jit_solution(10662884326438405606)
XLA Ops:
  0.6 69.0 %shard_map.94 = (bf16[160,768]{1,0:T(8,128)(2,1)}, f32[2,160,128]{2,1,0:T(8,128)}) custom-call(bf16[160,768]{1,0:T(8,128)(2,1)} %bitcast.4, bf16[3,160,1280]{2,1,0:T(8,128)(2,1)} %bitcast.3, bf16[160]{0:T(256)(128)(2,1)} %bias_ref.1, bf16[160,3584]{1,0:T(8,128)(2,1)} %adapter_hbm.1, bf16[384,3584]{1,0:T(8,128)(2,1)} %prompt_hbm.1, s32[384]{0:T(512)} %index_ref.1, ...), custom_call_target="tpu_custom_call" | custom-call | tf_op jit(solution)/shard_map/pallas_call | solution.py:499
  69.6 1.8 %shard_map.95 = (bf16[160,768]{1,0:T(8,128)(2,1)}, f32[160,112]{1,0:T(8,128)}, f32[3,40,160]{2,1,0:T(8,128)}) custom-call(bf16[160,768]{1,0:T(8,128)(2,1)} %get-tuple-element.8.hidden_in, f32[2,160,128]{2,1,0:T(8,128)} %get-tuple-element.9.sums_ref), custom_call_target="tpu_custom_call" | custom-call | tf_op jit(solution)/shard_map/pallas_call | solution.py:553

commit v4 on v3

--- a/solution.py
+++ b/solution.py
@@ -18,7 +18,8 @@
 WIDTH = 3584
 CAP = 24
 LOW = 128
-ECOL, EPAD = WIDTH // N_DP, 128
+ECOL = WIDTH // N_DP
+QUARTER = WIDTH // NX
 TAPC = 40
 GRAD_SCALE = 1.0 / math.sqrt(TOK * N_DP)
 
@@ -78,11 +79,14 @@
 def kernel(
     frames_hbm, weight_hbm, bias_ref, adapter_hbm, prompt_hbm, index_ref, clips_ref,
     hidden_ref, sums_ref,
-    frames_ref, weight_ref, adapter_ref, prompt_ref, in_sem, halving,
-    preact_ref, back_ref, prompt_pad, weight_t, weight_in, weight_own, xown, xbuf,
+    frames_all, weight_ref, adapter_ref, prompt_ref, in_sem, halving,
+    preact_ref, back_ref, weight_t, weight_in, weight_own, xbuf,
     slow, shigh, dlow, dhigh, send, got, slope_all,
-    parts, rs_in, rs_out, zsend, zgot, totals,
-    route_ss, route_rs, ag_ss, ag_rs, w_ss, w_rs, rs_ss, rs_rs, z_ss, z_rs,
+    columns_in, hidden_all, adapter_quarter, adapter_sum,
+    parts, rs_in, rs_out, conv_sum, conv_send, conv_got, conv_relay,
+    parts_got, parts_relay, parts_sum, parts_send, parts_last,
+    adapter_send, adapter_got, adapter_relay,
+    route_ss, route_rs, ag_ss, ag_rs, w_ss, w_rs, rs_ss, rs_rs, z_ss, z_rs, x_ss, x_rs,
 ):
     d = lax.axis_index("dp")
     f = lax.axis_index("fsdp")
@@ -93,9 +97,12 @@
         pltpu.make_async_copy(src, dst, in_sem.at[k])
         for k, (src, dst) in enumerate(
             (
-                (frames_hbm, frames_ref),
+                (frames_hbm, frames_all.at[f]),
+                *(
+                    (prompt_hbm.at[:, pl.ds(QUARTER * q, QUARTER)], prompt_ref.at[q])
+                    for q in range(NX)
+                ),
                 (adapter_hbm, adapter_ref),
-                (prompt_hbm, prompt_ref),
                 (weight_hbm, weight_ref),
             )
         )
@@ -137,50 +144,64 @@
     lax.fori_loop(1, N_DP, greet_dp, 0)
     lax.fori_loop(1, N_FSDP, greet_fsdp, 0)
 
+    pl.semaphore_wait(barrier, N_DP - 1 + N_FSDP - 1)
+
+    yr, yl, yo = lax.rem(y + 1, NY), lax.rem(y + NY - 1, NY), lax.rem(y + 2, NY)
+    mate = at(d, y * 2 + 1 - c)
+
+    class Gather:
+        def __init__(self, which, own, buf):
+            self.ss, self.rs = ag_ss.at[which], ag_rs.at[which]
+            self.own, self.buf = own, buf
+
+        def send(self, src, dst, k, dev):
+            go(src, dst, self.ss.at[k], self.rs.at[k], dev)
+
+        def half(self, g, h):
+            return self.buf.at[g, pl.ds(80 * h, 80)]
+
+        def come(self, dst, k):
+            arrived(dst, self.ss.at[k], self.rs.at[k])
+
+        def first(self):
+            for h in range(2):
+                for k, (to, part) in enumerate(((yr, h), (yl, 1 - h))):
+                    src = self.own.at[pl.ds(80 * part, 80)]
+                    self.send(src, self.half(f, part), 2 * k + part, at(d, to * 2 + c))
+            self.send(self.own, self.buf.at[f], 6, mate)
+
+        def relay(self):
+            for k, (come, to) in enumerate(((yl, yr), (yr, yl))):
+                block = self.half(come * 2 + c, k)
+                self.come(block, 2 * k + k)
+                self.send(block, block, 4 + k, at(d, to * 2 + c))
+
+        def near(self):
+            for k, come in enumerate((yl, yr)):
+                self.come(self.half(come * 2 + c, 1 - k), 2 * k + 1 - k)
+                block = self.buf.at[come * 2 + c]
+                self.send(block, block, 7 + k, mate)
+
+        def far(self):
+            for h in range(2):
+                block = self.half(yo * 2 + c, h)
+                self.come(block, 4 + h)
+                self.send(block, block, 9 + h, mate)
+
+        def from_mate(self, k):
+            o = 1 - c
+            if k < 3:
+                self.come(self.buf.at[(y, yl, yr)[k] * 2 + o], 6 + k)
+            else:
+                self.come(self.half(yo * 2 + o, 0), 9)
+                self.come(self.half(yo * 2 + o, 1), 10)
+
+    frames_ag = Gather(0, frames_hbm, frames_all)
+    frames_ag.first()
+
     row = iota((256, 256), 0)
     col = iota((256, 256), 1)
     halving[...] = pick(row == jnp.where(col < 128, 2 * col + 1, 2 * (col - 128))).astype(BF16)
-    loads[0].wait()
-    for b in range(3):
-        lines = nn(frames_ref[:, 256 * b : 256 * b + 256], halving[...])
-        for q in range(4):
-            quarter = lines[TAPC * q : TAPC * q + TAPC]
-            xown[q, :, 128 * b : 128 * b + 128] = jnp.concatenate(
-                [quarter[:, :128], quarter[:, 128:]], axis=0
-            ).astype(BF16)
-
-    pl.semaphore_wait(barrier, N_DP - 1 + N_FSDP - 1)
-
-    yr, yl, yo = lax.rem(y + 1, NY), lax.rem(y + NY - 1, NY), lax.rem(y + 2, NY)
-    mate = at(d, y * 2 + 1 - c)
-
-    class Gather:
-        def __init__(self, which, own, block):
-            self.ss, self.rs = ag_ss.at[which], ag_rs.at[which]
-            self.own, self.block = own, block
-            self.order = (yl, yr, yo)
-
-        def send(self, src, dst, k, dev):
-            go(src, dst, self.ss.at[k], self.rs.at[k], dev)
-
-        def first(self):
-            here = self.block(f)
-            for k, to in enumerate((yr, yl, yo)):
-                self.send(self.own, here, k, at(d, to * 2 + c))
-            self.send(self.own, here, 3, mate)
-
-        def forward(self, k):
-            block = self.block(self.order[k] * 2 + c)
-            arrived(block, self.ss.at[k], self.rs.at[k])
-            self.send(block, block, 4 + k, mate)
-
-        def from_mate(self, k):
-            come = y if k == 3 else self.order[k - 4]
-            arrived(self.block(come * 2 + 1 - c), self.ss.at[k], self.rs.at[k])
-
-    frames_ag = Gather(0, xown, lambda g: xbuf.at[pl.ds(4 * g, 4), pl.ds(0, 80), :])
-    frames_ag.first()
-    xbuf[pl.ds(4 * f, 4), pl.ds(0, 80), :] = xown[...]
 
     index = index_ref[...].reshape(1, TOK)
     group = iota((N_DP, TOK), 0)
@@ -201,9 +222,13 @@
     marks = jnp.where(part == 6, high_bits[:, None, :], jnp.where(part == 7, low_bits[:, None, :], 0.0))
     extra = nt(marks.reshape(N_DP * 8, TOK).astype(BF16), by_rank)
 
-    loads[1].wait()
-    loads[2].wait()
-    back_t = nt(adapter_ref[...], prompt_ref[...]).astype(BF16)
+    for q in range(NX):
+        loads[1 + q].wait()
+    loads[5].wait()
+    back_t = nt(adapter_ref[:, :QUARTER], prompt_ref[0])
+    for q in range(1, NX):
+        back_t = back_t + nt(adapter_ref[:, QUARTER * q : QUARTER * q + QUARTER], prompt_ref[q])
+    back_t = back_t.astype(BF16)
     send[0] = pack(slow, shigh, back_t, extra)
 
     def route(which):
@@ -242,7 +267,18 @@
 
     route(0)
 
-    loads[3].wait()
+    xr, xl, xo = lax.rem(x + 1, NX), lax.rem(x + NX - 1, NX), lax.rem(x + 2, NX)
+    x_order = ((1, xr), (3, xl), (2, xo))
+    half = pl.ds(pl.multiple_of(192 * c, 192), 192)
+    other_half = pl.ds(pl.multiple_of(192 - 192 * c, 192), 192)
+    for k, to in x_order:
+        go(
+            prompt_ref.at[to, half],
+            columns_in.at[k, half],
+            x_ss.at[0, k], x_rs.at[0, k], at(to * NZ + z, f),
+        )
+
+    loads[6].wait()
     pad8 = jnp.zeros((CH, 8), BF16)
     for o in range(N_DP):
         lines = [weight_ref[k, :, TAPC * o : TAPC * o + TAPC] for k in (2, 1, 0)]
@@ -254,33 +290,36 @@
     for k in range(6):
         inside = jnp.where(lane == start, 0.0, inside)
         start = start + clips_ref[0, k]
-    live = pick(iota((48, TOK), 0) < TAPC) * inside
+    pad_rows = jnp.zeros((8, TOK), F32)
 
     bias = bias_ref[...].astype(F32).reshape(1, CH)
     bias = jnp.sum(jnp.where(iota((CH, CH), 0) == iota((CH, CH), 1), bias, 0.0), axis=1, keepdims=True)
     preact_ref[...] = jnp.broadcast_to(bias, (CH, TOK))
 
     def preact_block(g):
+        lines = [
+            nn(frames_all[pl.ds(g, 1), :, 256 * b : 256 * b + 256][0], halving[...]) for b in range(3)
+        ]
+        odd = jnp.concatenate([part[:, :128] for part in lines], axis=1)
+        even = jnp.concatenate([part[:, 128:] for part in lines], axis=1)
+        early = pltpu.roll(odd, 1, 1) * inside
+        blocks = []
         for q in range(4):
-            lines = xbuf[pl.ds(4 * g + q, 1), pl.ds(0, 48), :][0].astype(F32)
-            early = (pltpu.roll(lines, 1, 1) * live).astype(BF16)
-            xbuf[pl.ds(4 * g + q, 1), pl.ds(80, 48), :] = early[None]
-        block = xbuf[pl.ds(4 * g, 4)].reshape(512, TOK)
+            rows = slice(TAPC * q, TAPC * q + TAPC)
+            blocks += [odd[rows], even[rows], early[rows], pad_rows]
+        block = jnp.concatenate(blocks, axis=0).astype(BF16)
+        xbuf[pl.ds(4 * g, 4)] = block.reshape(4, 128, TOK)
         preact_ref[...] += nn(weight_t[:, pl.ds(pl.multiple_of(g * 512, 512), 512)], block)
 
+    loads[0].wait()
     preact_block(f)
-    for k in range(2):
-        frames_ag.forward(k)
-    frames_ag.from_mate(3)
+    frames_ag.relay()
+    frames_ag.from_mate(0)
     preact_block(y * 2 + 1 - c)
-
-    for o in range(N_DP // 2):
-        columns = prompt_ref[:, ECOL * o : ECOL * o + ECOL]
-        prompt_pad[:, 128 * o : 128 * o + 128] = jnp.concatenate(
-            [columns, jnp.zeros((TOK, 128 - ECOL), BF16)], axis=1
-        )
-
-    frames_ag.forward(2)
+    frames_ag.near()
+    preact_block(yl * 2 + c)
+    preact_block(yr * 2 + c)
+    frames_ag.far()
 
     def weight_out(k, carry):
         to = lax.rem(f + k, N_FSDP)
@@ -293,8 +332,7 @@
     lax.fori_loop(1, N_FSDP, weight_out, 0)
     weight_in[pl.ds(f, 1)] = weight_t[:, pl.ds(pl.multiple_of(f * 512, 512), 512)][None]
 
-    for k in range(3):
-        preact_block(frames_ag.order[k] * 2 + c)
+    preact_block(yo * 2 + c)
 
     routed(0)
     tags = got[0, :, CAP:, :].astype(F32)
@@ -316,9 +354,9 @@
         dhigh[g] = token_hot(8, 6 * g, 6)
     back_ref[...] = unpack(dlow, dhigh, got[0])
 
-    for k in range(3):
-        frames_ag.from_mate(4 + k)
-        preact_block(frames_ag.order[k] * 2 + 1 - c)
+    for k, come in ((1, yl), (2, yr), (3, yo)):
+        frames_ag.from_mate(k)
+        preact_block(come * 2 + 1 - c)
 
     preact = preact_ref[...]
     cumul = 0.5 * (1.0 + lax.erf(preact * (1.0 / math.sqrt(2.0))))
@@ -329,98 +367,136 @@
     slope = cumul + preact * jnp.exp(-0.5 * preact * preact) * (1.0 / math.sqrt(2.0 * math.pi))
     slope_t = (back_ref[...] * slope).astype(BF16)
     slope_all[pl.ds(f, 1)] = slope_t[None]
-    slope_ag = Gather(1, slope_all.at[f], lambda g: slope_all.at[g])
+    slope_ag = Gather(1, slope_all.at[f], slope_all)
     slope_ag.first()
 
-    xr, xl, xo = lax.rem(x + 1, NX), lax.rem(x + NX - 1, NX), lax.rem(x + 2, NX)
     to_right, to_left = at(xr * NZ + z, f), at(xl * NZ + z, f)
 
-    def halves(which, owner, h):
-        return parts.at[which, pl.ds(owner * NZ + 4 * h, 4)]
-
-    def rs_send(which, src, k, dev):
-        go(src, rs_in.at[which, k], rs_ss.at[which, k], rs_rs.at[which, k], dev)
-
-    def rs_wait(which, k):
-        arrived(rs_in.at[which, k], rs_ss.at[which, k], rs_rs.at[which, k])
-
-    def rs_first(which, part):
-        part(xo, 0)
-        rs_send(which, halves(which, xo, 0), 0, to_right)
-        part(xo, 1)
-        rs_send(which, halves(which, xo, 1), 1, to_left)
-        part(xr, 1)
-        rs_send(which, halves(which, xr, 1), 2, to_right)
-        part(xl, 0)
-        rs_send(which, halves(which, xl, 0), 3, to_left)
-        part(xr, 0)
-        part(xl, 1)
-
-    def rs_second(which):
-        rs_wait(which, 0)
-        rs_out[which, 0] = (halves(which, xr, 0)[...].astype(F32) + rs_in[which, 0].astype(F32)).astype(BF16)
-        rs_send(which, rs_out.at[which, 0], 4, to_right)
-        rs_wait(which, 1)
-        rs_out[which, 1] = (halves(which, xl, 1)[...].astype(F32) + rs_in[which, 1].astype(F32)).astype(BF16)
-        rs_send(which, rs_out.at[which, 1], 5, to_left)
-
-    def rs_third(which):
-        for k in (2, 3, 4, 5):
-            rs_wait(which, k)
-        for h, (one, two) in enumerate(((4, 3), (5, 2))):
-            total = halves(which, x, h)[...].astype(F32) + rs_in[which, one].astype(F32)
-            total = total + rs_in[which, two].astype(F32)
-            totals[which, pl.ds(4 * h, 4)] = total
-            zsend[which, pl.ds(4 * h, 4)] = total.astype(BF16)
-
-        def step(k, carry):
-            to = lax.rem(z + k, NZ)
-            rcopy(
-                zsend.at[which, to], zgot.at[which, k],
-                z_ss.at[which, k], z_rs.at[which, k], at(x * NZ + to, f),
-            ).start()
-            return carry
-
-        lax.fori_loop(1, NZ, step, 0)
-
-    def rs_last(which):
-        total = totals[which, pl.ds(z, 1)][0]
-        for k in range(1, NZ):
-            arrived(zgot.at[which, k], z_ss.at[which, k], z_rs.at[which, k])
-            total = total + zgot[which, k].astype(F32)
-        return total * GRAD_SCALE
-
-    def store_parts(which, g, block):
-        for q in range(4):
-            parts[which, pl.ds(4 * g + q, 1)] = block[:, 128 * q : 128 * q + 128].astype(BF16)[None]
+    def halves(owner, h):
+        return parts.at[owner, pl.ds(4 * h, 4), pl.ds(0, 80)]
+
+    def rs_send(src, k, dev):
+        go(src, rs_in.at[k], rs_ss.at[k], rs_rs.at[k], dev)
+
+    def rs_wait(k):
+        arrived(rs_in.at[k], rs_ss.at[k], rs_rs.at[k])
 
     def conv_part(owner, h):
         g = 2 * owner + h
-        store_parts(0, g, nt(slope_t, xbuf[pl.ds(4 * g, 4)].reshape(512, TOK)))
-
-    def adapter_part(owner, h):
-        g = 2 * owner + h
-        store_parts(1, g, nn(hidden_pos, prompt_pad[:, pl.ds(pl.multiple_of(g * 512, 512), 512)]))
-
-    rs_first(0, conv_part)
-    for o in range(N_DP // 2, N_DP):
-        columns = prompt_ref[:, ECOL * o : ECOL * o + ECOL]
-        prompt_pad[:, 128 * o : 128 * o + 128] = jnp.concatenate(
-            [columns, jnp.zeros((TOK, 128 - ECOL), BF16)], axis=1
-        )
+        block = nt(slope_t, xbuf[pl.ds(4 * g, 4)].reshape(512, TOK))
+        for q in range(4):
+            parts[pl.ds(owner, 1), 4 * h + q] = block[:, 128 * q : 128 * q + 128].astype(BF16)[None]
+
+    def rs_second():
+        for k, owner, dev in ((0, xr, to_right), (1, xl, to_left)):
+            rs_wait(k)
+            total = halves(owner, k)[...].astype(F32) + rs_in[k].astype(F32)
+            rs_out[k] = total.astype(BF16)
+            rs_send(rs_out.at[k], 4 + k, dev)
+
+    def rs_third():
+        for k in (2, 3, 4, 5):
+            rs_wait(k)
+        for h, (one, two) in enumerate(((4, 3), (5, 2))):
+            total = halves(x, h)[...].astype(F32) + rs_in[one].astype(F32)
+            total = total + rs_in[two].astype(F32)
+            conv_sum[pl.ds(4 * h, 4)] = total
+            conv_send[pl.ds(4 * h, 4)] = total.astype(BF16)
+
+    def z_at(offset):
+        return lax.rem(z + NZ + offset, NZ)
+
+    class ZSum:
+        def __init__(self, which, chunk, value, dst, relay):
+            self.ss, self.rs = z_ss.at[which], z_rs.at[which]
+            self.chunk, self.value, self.dst, self.relayed = chunk, value, dst, relay
+
+        def send(self, src, slot, to):
+            go(src, self.dst.at[slot], self.ss.at[slot], self.rs.at[slot], at(x * NZ + z_at(to), f))
+
+        def wait(self, slot):
+            arrived(self.dst.at[slot], self.ss.at[slot], self.rs.at[slot])
+            return self.dst[slot].astype(F32)
+
+        def first(self):
+            for slot, chunk, to in ((5, -4, -2), (6, -3, -1), (7, 3, 1), (1, 1, 1), (2, -1, -1)):
+                self.send(self.chunk(z_at(chunk)), slot, to)
+
+        def relay(self):
+            total = self.value(z_at(-2)) + self.wait(5) + self.wait(6)
+            self.relayed[0] = total.astype(BF16)
+            self.send(self.relayed.at[0], 3, -2)
+            self.relayed[1] = (self.value(z_at(2)) + self.wait(7)).astype(BF16)
+            self.send(self.relayed.at[1], 4, 2)
+
+        def total(self):
+            total = self.value(z)
+            for slot in (1, 2, 4, 3):
+                total = total + self.wait(slot)
+            return total
+
+    z_conv = ZSum(
+        0, lambda t: conv_send.at[t], lambda t: conv_sum[pl.ds(t, 1)][0], conv_got, conv_relay
+    )
+    z_parts = ZSum(
+        1,
+        lambda t: parts.at[:, t, pl.ds(80, 80)],
+        lambda t: parts[:, pl.ds(t, 1), 80:160, :][:, 0].astype(F32),
+        parts_got,
+        parts_relay,
+    )
+    z_adapter = ZSum(
+        2, lambda t: adapter_send.at[t], lambda t: adapter_sum[pl.ds(t, 1)][0], adapter_got, adapter_relay
+    )
+
+    for k, (owner, h, dev) in enumerate(
+        ((xo, 0, to_right), (xo, 1, to_left), (xr, 1, to_right), (xl, 0, to_left))
+    ):
+        conv_part(owner, h)
+        rs_send(halves(owner, h), k, dev)
+    conv_part(xr, 0)
+    conv_part(xl, 1)
     conv_part(x, 0)
     conv_part(x, 1)
+    z_parts.first()
+
+    for k, to in x_order:
+        block = columns_in.at[k, half]
+        arrived(block, x_ss.at[0, k], x_rs.at[0, k])
+        go(block, block, x_ss.at[1, k], x_rs.at[1, k], mate)
+    rs_second()
 
     routed(1)
-    hidden_pos = unpack(slow, shigh, got[1]).astype(BF16)
-    rs_first(1, adapter_part)
-    rs_second(0)
-    for k in range(3):
-        slope_ag.forward(k)
-    adapter_part(x, 0)
-    adapter_part(x, 1)
-    rs_third(0)
-    rs_second(1)
+    hidden_all[0] = unpack(slow, shigh, got[1]).astype(BF16)
+    for k, to in x_order:
+        go(hidden_all.at[0], hidden_all.at[k], x_ss.at[2, k], x_rs.at[2, k], at(to * NZ + z, f))
+    adapter_quarter[...] = nn(hidden_all[0], prompt_ref[pl.ds(x, 1)][0])
+    slope_ag.relay()
+    slope_ag.near()
+    for k, to in x_order:
+        arrived(columns_in.at[k, other_half], x_ss.at[1, k], x_rs.at[1, k])
+    rs_third()
+    z_conv.first()
+    z_parts.relay()
+
+    for k, to in x_order[:2]:
+        arrived(hidden_all.at[k], x_ss.at[2, k], x_rs.at[2, k])
+        adapter_quarter[...] += nn(hidden_all[k], columns_in[k])
+    k = x_order[2][0]
+    arrived(hidden_all.at[k], x_ss.at[2, k], x_rs.at[2, k])
+    quarter = adapter_quarter[...] + nn(hidden_all[k], columns_in[k])
+    for q in range(NZ):
+        chunk = quarter[:, ECOL * q : ECOL * q + ECOL]
+        chunk = jnp.concatenate([chunk, jnp.zeros((CH, 128 - ECOL), F32)], axis=1)
+        adapter_sum[q] = chunk
+        adapter_send[q] = chunk.astype(BF16)
+    z_adapter.first()
+    z_conv.relay()
+    lines = z_parts.total()
+    parts_sum[...] = lines
+    parts_send[...] = lines.astype(BF16)
+    for k, to in x_order:
+        go(parts_send.at[to], parts_last.at[k], x_ss.at[3, k], x_rs.at[3, k], at(to * NZ + z, f))
 
     def weight_come(k, carry):
         come = lax.rem(f + N_FSDP - k, N_FSDP)
@@ -432,9 +508,9 @@
     lax.fori_loop(1, N_FSDP, weight_come, 0)
     for g in range(N_FSDP):
         weight_own[:, CH * g : CH * g + CH] = weight_in[g].T
-    rs_third(1)
-
-    for k in range(3, 7):
+    z_adapter.relay()
+    slope_ag.far()
+    for k in range(4):
         slope_ag.from_mate(k)
     grads = nn(weight_own[...], slope_all[...].reshape(N_FSDP * CH, TOK))
     odd, even = [], []
@@ -450,8 +526,13 @@
         )
         hidden_ref[:, 256 * b : 256 * b + 256] = nt(both, halving[...]).astype(BF16)
 
-    sums_ref[0] = rs_last(0)
-    sums_ref[1] = rs_last(1)
+    sums_ref[0, :80] = z_conv.total() * GRAD_SCALE
+    total = parts_sum[pl.ds(x, 1)][0]
+    for k, to in x_order:
+        arrived(parts_last.at[k], x_ss.at[3, k], x_rs.at[3, k])
+        total = total + parts_last[k].astype(F32)
+    sums_ref[0, 80:] = total * GRAD_SCALE
+    sums_ref[1] = z_adapter.total() * GRAD_SCALE
 
     for copy in pending:
         copy.wait_send()
@@ -467,17 +548,6 @@
         return carry
 
     lax.fori_loop(1, N_FSDP, weight_sent, 0)
-
-    def z_sent(k, carry):
-        to = lax.rem(z + k, NZ)
-        for which in range(2):
-            rcopy(
-                zsend.at[which, to], zgot.at[which, k],
-                z_ss.at[which, k], z_rs.at[which, k], at(x * NZ + to, f),
-            ).wait_send()
-        return carry
-
-    lax.fori_loop(1, NZ, z_sent, 0)
 
 
 def finish(hidden_in, sums_ref, hidden_ref, gadapter_ref, gconv_ref):
@@ -505,19 +575,17 @@
         in_specs=[hbm, hbm, vmem, hbm, hbm, vmem, smem],
         out_specs=(vmem, vmem),
         scratch_shapes=[
-            pltpu.VMEM((CH, 2 * TOK), BF16),
+            pltpu.VMEM((N_FSDP, CH, 2 * TOK), BF16),
             pltpu.VMEM((3, CH, N_FSDP * CH), BF16),
             pltpu.VMEM((CH, WIDTH), BF16),
-            pltpu.VMEM((TOK, WIDTH), BF16),
-            dma((4,)),
+            pltpu.VMEM((NX, TOK, QUARTER), BF16),
+            dma((7,)),
             pltpu.VMEM((256, 256), BF16),
             pltpu.VMEM((CH, TOK), F32),
             pltpu.VMEM((CH, TOK), F32),
-            pltpu.VMEM((TOK, N_DP * EPAD), BF16),
             pltpu.VMEM((CH, N_DP * 128), BF16),
             pltpu.VMEM((N_FSDP, CH, 512), BF16),
             pltpu.VMEM((512, N_FSDP * CH), BF16),
-            pltpu.VMEM((4, 80, TOK), BF16),
             pltpu.VMEM((N_DP, 128, TOK), BF16),
             pltpu.VMEM((N_DP * CAP, TOK), BF16),
             pltpu.VMEM((4, N_DP * 8, TOK), BF16),
@@ -526,17 +594,31 @@
             pltpu.VMEM((2, N_DP, 32, 128), BF16),
             pltpu.VMEM((2, N_DP, 32, 128), BF16),
             pltpu.VMEM((N_FSDP, CH, TOK), BF16),
-            pltpu.VMEM((2, N_DP, CH, 128), BF16),
-            pltpu.VMEM((2, 6, 4, CH, 128), BF16),
-            pltpu.VMEM((2, 2, 4, CH, 128), BF16),
-            pltpu.VMEM((2, NZ, CH, 128), BF16),
-            pltpu.VMEM((2, NZ, CH, 128), BF16),
-            pltpu.VMEM((2, NZ, CH, 128), F32),
+            pltpu.VMEM((NX, TOK, QUARTER), BF16),
+            pltpu.VMEM((NX, CH, TOK), BF16),
+            pltpu.VMEM((CH, QUARTER), F32),
+            pltpu.VMEM((NZ, CH, 128), F32),
+            pltpu.VMEM((NX, NZ, CH, 128), BF16),
+            pltpu.VMEM((6, 4, 80, 128), BF16),
+            pltpu.VMEM((2, 4, 80, 128), BF16),
+            pltpu.VMEM((NZ, 80, 128), F32),
+            pltpu.VMEM((NZ, 80, 128), BF16),
+            pltpu.VMEM((NZ, 80, 128), BF16),
+            pltpu.VMEM((2, 80, 128), BF16),
+            pltpu.VMEM((NZ, NX, 80, 128), BF16),
+            pltpu.VMEM((2, NX, 80, 128), BF16),
+            pltpu.VMEM((NX, 80, 128), F32),
+            pltpu.VMEM((NX, 80, 128), BF16),
+            pltpu.VMEM((NX, 80, 128), BF16),
+            pltpu.VMEM((NZ, CH, 128), BF16),
+            pltpu.VMEM((NZ, CH, 128), BF16),
+            pltpu.VMEM((2, CH, 128), BF16),
             dma((2, N_DP)), dma((2, N_DP)),
-            dma((2, 7)), dma((2, 7)),
+            dma((2, 11)), dma((2, 11)),
             dma((N_FSDP,)), dma((N_FSDP,)),
-            dma((2, 6)), dma((2, 6)),
-            dma((2, NZ)), dma((2, NZ)),
+            dma((6,)), dma((6,)),
+            dma((3, NZ)), dma((3, NZ)),
+            dma((4, NX)), dma((4, NX)),
         ],
         compiler_params=pltpu.CompilerParams(
             collective_id=0, has_side_effects=True, vmem_limit_bytes=56 * 1024 * 1024

time: 72.4 us -> 63.6 us (0.88)
  Pallas kernels: 70.8 us -> 62.3 us
    pallas_call x1, Pallas kernels: 69 us -> 60.5 us  [body(): pl.pallas_call(kernel, out_shape=(jax.ShapeDtypeStruct((CH, 2 * TOK), BF1...]
where the time goes in v4:
time: 63.6 us; the launch traced here: 62.9 us
  Pallas kernels  62.3 us (98%)
  between operations  0.64 us (1%)
    pallas_call x1, Pallas kernels, body(): pl.pallas_call(kernel, out_shape=(jax.ShapeDtypeStruct((CH, 2 * TOK), BF1...  60.5 us
    pallas_call x1, Pallas kernels, body(): pl.pallas_call(finish, out_shape=(jax.ShapeDtypeStruct((CH, 2 * TOK), BF1...  1.81 us

profile of v4, /device:TPU:2, one launch (start us, length us, event | category | flops | bytes accessed | tf_op | source)
XLA Modules:
  0.0 62.9 jit_solution(8344140398308618171)
XLA Ops:
  0.6 60.5 %shard_map.94 = (bf16[160,768]{1,0:T(8,128)(2,1)}, f32[2,160,128]{2,1,0:T(8,128)}) custom-call(bf16[160,768]{1,0:T(8,128)(2,1)} %bitcast.4, bf16[3,160,1280]{2,1,0:T(8,128)(2,1)} %bitcast.3, bf16[160]{0:T(256)(128)(2,1)} %bias_ref.1, bf16[160,3584]{1,0:T(8,128)(2,1)} %adapter_hbm.1, bf16[384,3584]{1,0:T(8,128)(2,1)} %prompt_hbm.1, s32[384]{0:T(512)} %index_ref.1, ...), custom_call_target="tpu_custom_call" | custom-call | tf_op jit(solution)/shard_map/pallas_call | solution.py:569
  61.1 1.8 %shard_map.95 = (bf16[160,768]{1,0:T(8,128)(2,1)}, f32[160,112]{1,0:T(8,128)}, f32[3,40,160]{2,1,0:T(8,128)}) custom-call(bf16[160,768]{1,0:T(8,128)(2,1)} %get-tuple-element.8.hidden_in, f32[2,160,128]{2,1,0:T(8,128)} %get-tuple-element.9.sums_ref), custom_call_target="tpu_custom_call" | custom-call | tf_op jit(solution)/shard_map/pallas_call | solution.py:635

commit v5 on v4

--- a/solution.py
+++ b/solution.py
@@ -19,6 +19,8 @@
 CAP = 24
 LOW = 128
 ECOL = WIDTH // N_DP
+XROWS = 48
+ZROWS = CH - XROWS
 QUARTER = WIDTH // NX
 TAPC = 40
 GRAD_SCALE = 1.0 / math.sqrt(TOK * N_DP)
@@ -373,7 +375,7 @@
     to_right, to_left = at(xr * NZ + z, f), at(xl * NZ + z, f)
 
     def halves(owner, h):
-        return parts.at[owner, pl.ds(4 * h, 4), pl.ds(0, 80)]
+        return parts.at[owner, pl.ds(4 * h, 4), pl.ds(0, XROWS)]
 
     def rs_send(src, k, dev):
         go(src, rs_in.at[k], rs_ss.at[k], rs_rs.at[k], dev)
@@ -440,8 +442,8 @@
     )
     z_parts = ZSum(
         1,
-        lambda t: parts.at[:, t, pl.ds(80, 80)],
-        lambda t: parts[:, pl.ds(t, 1), 80:160, :][:, 0].astype(F32),
+        lambda t: parts.at[:, t, pl.ds(XROWS, ZROWS)],
+        lambda t: parts[:, pl.ds(t, 1), XROWS:, :][:, 0].astype(F32),
         parts_got,
         parts_relay,
     )
@@ -464,6 +466,7 @@
         block = columns_in.at[k, half]
         arrived(block, x_ss.at[0, k], x_rs.at[0, k])
         go(block, block, x_ss.at[1, k], x_rs.at[1, k], mate)
+
     rs_second()
 
     routed(1)
@@ -526,12 +529,12 @@
         )
         hidden_ref[:, 256 * b : 256 * b + 256] = nt(both, halving[...]).astype(BF16)
 
-    sums_ref[0, :80] = z_conv.total() * GRAD_SCALE
+    sums_ref[0, :XROWS] = z_conv.total() * GRAD_SCALE
     total = parts_sum[pl.ds(x, 1)][0]
     for k, to in x_order:
         arrived(parts_last.at[k], x_ss.at[3, k], x_rs.at[3, k])
         total = total + parts_last[k].astype(F32)
-    sums_ref[0, 80:] = total * GRAD_SCALE
+    sums_ref[0, XROWS:] = total * GRAD_SCALE
     sums_ref[1] = z_adapter.total() * GRAD_SCALE
 
     for copy in pending:
@@ -599,17 +602,17 @@
             pltpu.VMEM((CH, QUARTER), F32),
             pltpu.VMEM((NZ, CH, 128), F32),
             pltpu.VMEM((NX, NZ, CH, 128), BF16),
-            pltpu.VMEM((6, 4, 80, 128), BF16),
-            pltpu.VMEM((2, 4, 80, 128), BF16),
-            pltpu.VMEM((NZ, 80, 128), F32),
-            pltpu.VMEM((NZ, 80, 128), BF16),
-            pltpu.VMEM((NZ, 80, 128), BF16),
-            pltpu.VMEM((2, 80, 128), BF16),
-            pltpu.VMEM((NZ, NX, 80, 128), BF16),
-            pltpu.VMEM((2, NX, 80, 128), BF16),
-            pltpu.VMEM((NX, 80, 128), F32),
-            pltpu.VMEM((NX, 80, 128), BF16),
-            pltpu.VMEM((NX, 80, 128), BF16),
+            pltpu.VMEM((6, 4, XROWS, 128), BF16),
+            pltpu.VMEM((2, 4, XROWS, 128), BF16),
+            pltpu.VMEM((NZ, XROWS, 128), F32),
+            pltpu.VMEM((NZ, XROWS, 128), BF16),
+            pltpu.VMEM((NZ, XROWS, 128), BF16),
+            pltpu.VMEM((2, XROWS, 128), BF16),
+            pltpu.VMEM((NZ, NX, ZROWS, 128), BF16),
+            pltpu.VMEM((2, NX, ZROWS, 128), BF16),
+            pltpu.VMEM((NX, ZROWS, 128), F32),
+            pltpu.VMEM((NX, ZROWS, 128), BF16),
+            pltpu.VMEM((NX, ZROWS, 128), BF16),
             pltpu.VMEM((NZ, CH, 128), BF16),
             pltpu.VMEM((NZ, CH, 128), BF16),
             pltpu.VMEM((2, CH, 128), BF16),

time: 63.6 us -> 62.3 us (0.980)
  Pallas kernels: 62.3 us -> 61.3 us
    pallas_call x1, Pallas kernels: 60.5 us -> 59.5 us  [body(): pl.pallas_call(kernel, out_shape=(jax.ShapeDtypeStruct((CH, 2 * TOK), BF1...]
where the time goes in v5:
time: 62.3 us; the launch traced here: 62 us
  Pallas kernels  61.3 us (98%)
  between operations  0.64 us (1%)
    pallas_call x1, Pallas kernels, body(): pl.pallas_call(kernel, out_shape=(jax.ShapeDtypeStruct((CH, 2 * TOK), BF1...  59.5 us
    pallas_call x1, Pallas kernels, body(): pl.pallas_call(finish, out_shape=(jax.ShapeDtypeStruct((CH, 2 * TOK), BF1...  1.81 us

profile of v5, /device:TPU:2, one launch (start us, length us, event | category | flops | bytes accessed | tf_op | source)
XLA Modules:
  0.0 62.0 jit_solution(2457265678848231916)
XLA Ops:
  0.6 59.5 %shard_map.94 = (bf16[160,768]{1,0:T(8,128)(2,1)}, f32[2,160,128]{2,1,0:T(8,128)}) custom-call(bf16[160,768]{1,0:T(8,128)(2,1)} %bitcast.4, bf16[3,160,1280]{2,1,0:T(8,128)(2,1)} %bitcast.3, bf16[160]{0:T(256)(128)(2,1)} %bias_ref.1, bf16[160,3584]{1,0:T(8,128)(2,1)} %adapter_hbm.1, bf16[384,3584]{1,0:T(8,128)(2,1)} %prompt_hbm.1, s32[384]{0:T(512)} %index_ref.1, ...), custom_call_target="tpu_custom_call" | custom-call | tf_op jit(solution)/shard_map/pallas_call | solution.py:572
  60.2 1.8 %shard_map.95 = (bf16[160,768]{1,0:T(8,128)(2,1)}, f32[160,112]{1,0:T(8,128)}, f32[3,40,160]{2,1,0:T(8,128)}) custom-call(bf16[160,768]{1,0:T(8,128)(2,1)} %get-tuple-element.8.hidden_in, f32[2,160,128]{2,1,0:T(8,128)} %get-tuple-element.9.sums_ref), custom_call_target="tpu_custom_call" | custom-call | tf_op jit(solution)/shard_map/pallas_call | solution.py:638

commit v6 on v5

--- a/solution.py
+++ b/solution.py
@@ -460,7 +460,6 @@
     conv_part(xl, 1)
     conv_part(x, 0)
     conv_part(x, 1)
-    z_parts.first()
 
     for k, to in x_order:
         block = columns_in.at[k, half]
@@ -473,6 +472,7 @@
     hidden_all[0] = unpack(slow, shigh, got[1]).astype(BF16)
     for k, to in x_order:
         go(hidden_all.at[0], hidden_all.at[k], x_ss.at[2, k], x_rs.at[2, k], at(to * NZ + z, f))
+    z_parts.first()
     adapter_quarter[...] = nn(hidden_all[0], prompt_ref[pl.ds(x, 1)][0])
     slope_ag.relay()
     slope_ag.near()

time: 62.3 us -> 69.3 us (1.11); the launches traced: 62 us -> 68.2 us
  Pallas kernels: 61.3 us -> 67.5 us
    pallas_call x1, Pallas kernels: 59.5 us -> 65.7 us  [body(): pl.pallas_call(kernel, out_shape=(jax.ShapeDtypeStruct((CH, 2 * TOK), BF1...]
where the time goes in v6:
time: 69.3 us; the launch traced here: 68.2 us
  Pallas kernels  67.5 us (97%)
    pallas_call x1, Pallas kernels, body(): pl.pallas_call(kernel, out_shape=(jax.ShapeDtypeStruct((CH, 2 * TOK), BF1...  65.7 us
    pallas_call x1, Pallas kernels, body(): pl.pallas_call(finish, out_shape=(jax.ShapeDtypeStruct((CH, 2 * TOK), BF1...  1.81 us

profile of v6, /device:TPU:2, one launch (start us, length us, event | category | flops | bytes accessed | tf_op | source)
XLA Modules:
  0.0 68.2 jit_solution(14792001795124502941)
XLA Ops:
  0.6 65.7 %shard_map.94 = (bf16[160,768]{1,0:T(8,128)(2,1)}, f32[2,160,128]{2,1,0:T(8,128)}) custom-call(bf16[160,768]{1,0:T(8,128)(2,1)} %bitcast.4, bf16[3,160,1280]{2,1,0:T(8,128)(2,1)} %bitcast.3, bf16[160]{0:T(256)(128)(2,1)} %bias_ref.1, bf16[160,3584]{1,0:T(8,128)(2,1)} %adapter_hbm.1, bf16[384,3584]{1,0:T(8,128)(2,1)} %prompt_hbm.1, s32[384]{0:T(512)} %index_ref.1, ...), custom_call_target="tpu_custom_call" | custom-call | tf_op jit(solution)/shard_map/pallas_call | solution.py:572
  66.4 1.8 %shard_map.95 = (bf16[160,768]{1,0:T(8,128)(2,1)}, f32[160,112]{1,0:T(8,128)}, f32[3,40,160]{2,1,0:T(8,128)}) custom-call(bf16[160,768]{1,0:T(8,128)(2,1)} %get-tuple-element.8.hidden_in, f32[2,160,128]{2,1,0:T(8,128)} %get-tuple-element.9.sums_ref), custom_call_target="tpu_custom_call" | custom-call | tf_op jit(solution)/shard_map/pallas_call | solution.py:638
